TPU v7x, 32 devices: a whole 2x2x4 slice. The times are simulated.
32 devices in a mesh: groups: 2 (over x), lon: 16 (over z, y, core).
Axes of the slice: x: 2, y: 2, z: 4, core: 2. Of those that a mesh axis runs over, the one named last changes fastest.
Arguments:
- fields: bfloat16 [32, 32, 1500], P(('groups', 'lon')), parts along dimension 0, may hold values from -6 to 6
- level_ids: int32 [6], P('groups'), parts along dimension 0, may hold values from 0 to 2, each once
- embed_weight: bfloat16 [500, 512], replicated, may hold values from -0.25 to 0.25
- level_embed: bfloat16 [3, 512], replicated, may hold values from -6 to 6
- enc_gain: float32 [512], replicated, may hold values from 0.1 to 1.9
- latent_query: bfloat16 [2, 512], replicated, may hold values from -0.049804688 to 0.049804688
- kv_weight: bfloat16 [512, 1024], replicated, may hold values from -0.25 to 0.25
- pool_out: bfloat16 [512, 512], replicated, may hold values from -0.25 to 0.25
- attn_gain: float32 [512], replicated, may hold values from 0.1 to 1.9
- qkv_weight: bfloat16 [512, 1536], replicated, may hold values from -0.25 to 0.25
- attn_proj: bfloat16 [512, 512], replicated, may hold values from -0.25 to 0.25
- mlp_gain: float32 [512], replicated, may hold values from 0.1 to 1.9
- mlp_up: bfloat16 [512, 2048], replicated, may hold values from -0.25 to 0.25
- mlp_down: bfloat16 [2048, 512], replicated, may hold values from -0.125 to 0.125
- level_mix: float32 [3, 2], replicated, may hold values from 0.25 to 4
- dec_gain: float32 [512], replicated, may hold values from 0.1 to 1.9
- dec_weight: bfloat16 [512, 500], replicated, may hold values from -0.25 to 0.25
Outputs:
- forecast: bfloat16 [32, 32, 1500], P(('groups', 'lon')), parts along dimension 0
There are 2 independent parts, one for each index of `groups`. A program takes and returns all parts, laid end to end along the dimension named above; an argument that names none is the same for every part. Nothing has to cross between parts.
Inputs may be any that keep to these rules, and one draw needn't show every extreme that they name: level_ids holds each of 0 to 2 once.
All inputs are finite; a program needn't handle non-finite values.
Results may differ from a plain program's by a relative error of at most 0.014.
Values may be sent and summed in bfloat16 or wider, within the bound.
No kernel may reach another device: no remote copies, remote signals or barrier semaphores. Data moves between devices by JAX's collectives and lax.ppermute only.
A program may use at most 128 MiB of HBM per device.

v0:
```python
import functools

import jax
import jax.numpy as jnp
from jax import lax
from jax.experimental import pallas as pl
from jax.experimental.pallas import tpu as pltpu
from jax.sharding import PartitionSpec as P

D = 512
HEADS = 8
HEAD_DIM = D // HEADS
PIN = 500
LEV = 3
LATL = 2
W_LAT = 4
W_LON = 8
STEPS = 2
ROW_PARTS = 4
MLP = 2048
PATCHES = W_LAT * W_LON
TOKENS = PATCHES * LATL
HALF = D // 2
PAIR = 2 * HEAD_DIM
EARLY, LATE = 11, 4
LANES = 128
LOAD_LIMIT = 56 * 1024 * 1024
MAIN_LIMIT = 56 * 1024 * 1024
EMBED_ROW, MIX_ROW, LATENT_ROW, GAIN_ROW, TABLE_ROWS = 0, 3, 9, 11, 16

norm_eps = 1e-05
head_eps = 1e-06

F32 = jnp.float32
BF16 = jnp.bfloat16


def mm(a, b):
    return jnp.dot(a, b, preferred_element_type=F32)


def mm_t(a, b):
    return lax.dot_general(a, b, (((1,), (1,)), ((), ())), preferred_element_type=F32)


def layer_norm(values, gain):
    average = jnp.mean(values, axis=-1, keepdims=True)
    centred = values - average
    spread = jnp.mean(centred * centred, axis=-1, keepdims=True)
    return centred * lax.rsqrt(spread + norm_eps) * gain


def iota(shape, dim):
    return lax.broadcasted_iota(jnp.int32, shape, dim)


def load_kernel(*refs):
    (
        ids_from,
        mix_from,
        level_embed_from,
        latent_query_from,
        enc_gain_from,
        attn_gain_from,
        mlp_gain_from,
        dec_gain_from,
        dec_from,
        embed_from,
        kv_from,
        pool_from,
        _,
        table_ref,
        query_ref,
        mean_ref,
        spread_ref,
        ones_ref,
        half_ref,
        allowed_ref,
        dec_ref,
        embed_ref,
        kv_ref,
        pool_ref,
        ids_ref,
        mix_ref,
        level_embed_ref,
        latent_query_ref,
        gain_refs,
        dec_rows_ref,
        arrivals,
    ) = refs
    pairs = [
        (ids_from, ids_ref),
        (mix_from, mix_ref),
        (level_embed_from, level_embed_ref),
        (latent_query_from, latent_query_ref),
        (enc_gain_from, gain_refs.at[0]),
        (attn_gain_from, gain_refs.at[1]),
        (mlp_gain_from, gain_refs.at[2]),
        (dec_gain_from, gain_refs.at[3]),
        (dec_from, dec_rows_ref),
        (embed_from, embed_ref),
        (kv_from, kv_ref),
        (pool_from, pool_ref),
    ]
    copies = [
        pltpu.make_async_copy(here, there, arrivals.at[i]) for i, (here, there) in enumerate(pairs)
    ]
    for copy in copies:
        copy.start()

    feature_head = iota((D, LANES), 0) // HEAD_DIM
    lane = iota((D, LANES), 1)
    on_head = (feature_head == lane % HEADS) & (lane < LATL * HEADS)
    mean_ref[...] = jnp.where(on_head, 1.0 / HEAD_DIM, 0.0).astype(BF16)
    spread_ref[...] = jnp.where(
        iota((LATL * HEADS, LATL * D), 0) == iota((LATL * HEADS, LATL * D), 1) // HEAD_DIM, 1.0, 0.0
    ).astype(BF16)
    ones_ref[...] = jnp.where(
        iota((HALF, HALF), 0) // HEAD_DIM == iota((HALF, HALF), 1) // HEAD_DIM, 1.0 / HEAD_DIM, 0.0
    ).astype(BF16)
    half_ref[...] = jnp.where(
        (iota((PAIR, PAIR), 0) < HEAD_DIM) == (iota((PAIR, PAIR), 1) < HEAD_DIM), 1.0, 0.0
    ).astype(BF16)
    row_bit = (iota((TOKENS, PAIR), 0) // 4) % 2
    lane_bit = (iota((TOKENS, PAIR), 1) // 4) % 2
    allowed_ref[...] = jnp.where(row_bit == lane_bit, 1.0, 0.0)

    for copy in copies[:8]:
        copy.wait()
    level_embed = level_embed_ref[...].astype(F32)
    for l in range(LEV):
        level = ids_ref[l]
        row = level_embed[LEV - 1 : LEV]
        for i in reversed(range(LEV - 1)):
            row = jnp.where(level == i, level_embed[i : i + 1], row)
        table_ref[EMBED_ROW + l : EMBED_ROW + l + 1, :] = row
        for j in range(LATL):
            at = MIX_ROW + l * LATL + j
            table_ref[at : at + 1, :] = jnp.full((1, D), mix_ref[j, level])
    latent = latent_query_ref[...].astype(F32)
    table_ref[LATENT_ROW : LATENT_ROW + LATL, :] = latent
    for i in range(4):
        table_ref[GAIN_ROW + i : GAIN_ROW + i + 1, :] = gain_refs[i]
    row_id = iota((LANES, D), 0)
    own_head = (row_id % HEADS) == iota((LANES, D), 1) // HEAD_DIM
    spots = jnp.zeros((LANES, D), F32)
    for j in range(LATL):
        mine = own_head & (row_id // HEADS == j)
        spots = jnp.where(mine, jnp.broadcast_to(latent[j : j + 1], (LANES, D)), spots)
    mean_square = jnp.sum(spots * spots, axis=-1, keepdims=True) / HEAD_DIM
    query_ref[...] = (spots * lax.rsqrt(mean_square + head_eps)).T.astype(BF16)

    copies[8].wait()
    dec_ref[...] = dec_rows_ref[...].astype(F32).T.astype(BF16)
    for copy in copies[9:]:
        copy.wait()


def load(after, scalars, rows, dec, early):
    far = pl.BlockSpec(memory_space=pl.ANY)
    made = [
        pltpu.VMEM((TABLE_ROWS, D), F32),
        pltpu.VMEM((D, LANES), BF16),
        pltpu.VMEM((D, LANES), BF16),
        pltpu.VMEM((LATL * HEADS, LATL * D), BF16),
        pltpu.VMEM((HALF, HALF), BF16),
        pltpu.VMEM((PAIR, PAIR), BF16),
        pltpu.VMEM((TOKENS, PAIR), F32),
        pltpu.VMEM(dec.shape[::-1], BF16),
    ] + [pltpu.VMEM(a.shape, a.dtype) for a in early]
    inputs = (*scalars, *rows, dec, *early)
    return pl.pallas_call(
        load_kernel,
        in_specs=[far] * (len(inputs) + 1),
        out_specs=[pl.BlockSpec(memory_space=pltpu.VMEM)] * len(made),
        out_shape=made,
        scratch_shapes=[pltpu.SMEM(a.shape, a.dtype) for a in scalars]
        + [
            pltpu.VMEM((LEV, D), BF16),
            pltpu.VMEM((LATL, D), BF16),
            pltpu.VMEM((4, 1, D), F32),
            pltpu.VMEM(dec.shape, BF16),
            pltpu.SemaphoreType.DMA((len(inputs),)),
        ],
        compiler_params=pltpu.CompilerParams(vmem_limit_bytes=LOAD_LIMIT),
        cost_estimate=pl.CostEstimate(flops=0, bytes_accessed=8_000_000, transcendentals=0),
    )(*inputs, after)


def forecast_kernel(windows, *refs):
    (
        table_ref,
        query_ref,
        mean_ref,
        spread_ref,
        ones_ref,
        half_ref,
        allowed_ref,
        dec_ref,
        embed_ref,
        kv_ref,
        pool_ref,
    ) = refs[:EARLY]
    far, (x_ref, out_ref), refs = refs[EARLY:][:LATE], refs[EARLY + LATE :][:2], refs[EARLY + LATE + 2 :]
    near, (state, wide, arrivals) = refs[:LATE], refs[LATE:]
    qkv_ref, proj_ref, up_ref, down_ref = near
    copies = [
        pltpu.make_async_copy(far[i], near[i], arrivals.at[i]) for i in range(LATE)
    ]

    def in_first_window(action):
        if windows == 1:
            action()
        else:
            pl.when(pl.program_id(0) == 0)(action)

    def start(*wanted):
        def action():
            for i in wanted:
                copies[i].start()

        in_first_window(action)

    def wait(turn_index, *wanted):
        def action():
            for i in wanted:
                copies[i].wait()

        if turn_index == 0:
            in_first_window(action)

    start(0, 1, 2, 3)

    def entry(at):
        return table_ref[at : at + 1, :]

    def embed(l):
        return entry(EMBED_ROW + l)

    def mixing(l, j):
        return entry(MIX_ROW + l * LATL + j)

    low = iota((1, PAIR), 1) < HEAD_DIM

    arrived = x_ref[0].astype(F32).reshape(PATCHES, LEV * PIN)
    for l in range(LEV):
        state[l * PATCHES : (l + 1) * PATCHES, :] = arrived[:, l * PIN : (l + 1) * PIN]

    def by_level(values):
        return [values[l * PATCHES : (l + 1) * PATCHES] for l in range(LEV)]

    for turn_index in range(STEPS):
        tokens = by_level(mm(state[...].astype(BF16), embed_ref[...]))
        tokens = jnp.concatenate([tokens[l] + embed(l) for l in range(LEV)], axis=0)
        tokens = layer_norm(tokens, entry(GAIN_ROW)).astype(BF16)
        keyval = mm(tokens, kv_ref[...])
        keys = keyval[:, :D]
        values = by_level(keyval[:, D:])
        mean_square = mm((keys * keys).astype(BF16), mean_ref[...])
        scores = mm(keys.astype(BF16), query_ref[...])
        scores = scores * lax.rsqrt(mean_square + head_eps) * HEAD_DIM ** (-0.5)
        scores = scores[:, : LATL * HEADS]
        parts = by_level(jnp.exp(scores))
        inverse = 1.0 / (parts[0] + parts[1] + parts[2])
        weights = jnp.concatenate([part * inverse for part in parts], axis=0).astype(BF16)
        wide_weights = by_level(mm(weights, spread_ref[...]))
        pooled = []
        for j in range(LATL):
            terms = [wide_weights[l][:, j * D : (j + 1) * D] * values[l] for l in range(LEV)]
            pooled.append(terms[0] + terms[1] + terms[2])
        latents = mm(jnp.concatenate(pooled, axis=0).astype(BF16), pool_ref[...])
        latents = jnp.concatenate(
            [
                latents[j * PATCHES : (j + 1) * PATCHES] + entry(LATENT_ROW + j)
                for j in range(LATL)
            ],
            axis=0,
        )
        normed = layer_norm(latents, entry(GAIN_ROW + 1)).astype(BF16)
        wait(turn_index, 0)
        projected = mm(normed, qkv_ref[...])
        allowed = allowed_ref[...]
        if windows > 1:
            cut = jnp.where(pl.program_id(0) == windows - 1, 1.0, 0.0)
            allowed = 1.0 - cut * (1.0 - allowed)
        halves = jnp.concatenate(
            [projected[:, i * HALF : (i + 1) * HALF] for i in range(4)], axis=0
        )
        mean_square = mm((halves * halves).astype(BF16), ones_ref[...])
        halves = halves * lax.rsqrt(mean_square + head_eps)
        win_values = projected[:, 2 * D :]
        mixed = []
        for pair in range(HEADS // 2):
            half, at = pair // 2, (pair % 2) * PAIR
            query = halves[half * TOKENS : (half + 1) * TOKENS, at : at + PAIR].astype(BF16)
            key = halves[(2 + half) * TOKENS : (3 + half) * TOKENS, at : at + PAIR]
            value = win_values[:, pair * PAIR : (pair + 1) * PAIR]
            key = jnp.concatenate(
                [jnp.where(low, key, 0.0), jnp.where(low, 0.0, key)], axis=0
            ).astype(BF16)
            value = jnp.concatenate(
                [jnp.where(low, value, 0.0), jnp.where(low, 0.0, value)], axis=0
            ).astype(BF16)
            weights = jnp.exp(mm_t(query, key) * HEAD_DIM ** (-0.5)) * allowed
            both = mm(weights.astype(BF16), jnp.concatenate([value, half_ref[...]], axis=1))
            mixed.append((both[:, :PAIR] / both[:, PAIR:]).astype(BF16))
        wait(turn_index, 1)
        attended = latents + mm(jnp.concatenate(mixed, axis=1), proj_ref[...])
        normed = layer_norm(attended, entry(GAIN_ROW + 2)).astype(BF16)
        wait(turn_index, 2)
        hidden = jax.nn.gelu(mm(normed, up_ref[...])).astype(BF16)
        wait(turn_index, 3)
        backbone = attended + mm(hidden, down_ref[...])
        first, second = backbone[:PATCHES], backbone[PATCHES:]
        blended = jnp.concatenate(
            [mixing(l, 0) * first + mixing(l, 1) * second + embed(l) for l in range(LEV)], axis=0
        )
        normed = layer_norm(blended, entry(GAIN_ROW + 3)).astype(BF16)
        state[...] = (state[...] + mm(normed, dec_ref[...])).astype(BF16).astype(F32)

    for l in range(LEV):
        wide[:, l * PIN : (l + 1) * PIN] = state[l * PATCHES : (l + 1) * PATCHES, :]
    out_ref[0] = wide[...].reshape(out_ref.shape[1:]).astype(BF16)


def forecast(windows, arranged, early, late):
    vmem = pl.BlockSpec(memory_space=pltpu.VMEM)
    if windows == 1:
        block, grid = vmem, ()
    else:
        block = pl.BlockSpec((1,) + arranged.shape[1:], lambda i: (i, 0, 0, 0))
        grid = (windows,)
    early = [pltpu.with_memory_space_constraint(a, pltpu.VMEM) for a in early]
    return pl.pallas_call(
        functools.partial(forecast_kernel, windows),
        grid=grid,
        in_specs=[vmem] * EARLY + [pl.BlockSpec(memory_space=pl.ANY)] * LATE + [block],
        out_specs=block,
        out_shape=jax.ShapeDtypeStruct(arranged.shape, BF16),
        scratch_shapes=[pltpu.VMEM(a.shape, a.dtype) for a in late]
        + [
            pltpu.VMEM((LEV * PATCHES, PIN), F32),
            pltpu.VMEM((PATCHES, LEV * PIN), F32),
            pltpu.SemaphoreType.DMA((LATE,)),
        ],
        compiler_params=pltpu.CompilerParams(vmem_limit_bytes=MAIN_LIMIT),
    )(*early, *late, arranged)


def turn_kernel(step, direction, x_ref, out_ref, *token_ref):
    count = x_ref.shape[0] if len(x_ref.shape) == 3 else out_ref.shape[0]
    for ref in token_ref:
        ref[...] = jnp.zeros_like(ref)
    turned = lax.axis_index("lon") < step
    blocks = x_ref[...].astype(F32).reshape(count, 2, LEV * PIN)

    @pl.when(turned)
    def _():
        if direction > 0:
            moved = jnp.concatenate([blocks[1:], blocks[:1]], axis=0)
        else:
            moved = jnp.concatenate([blocks[-1:], blocks[:-1]], axis=0)
        out_ref[...] = moved.reshape(out_ref.shape).astype(BF16)

    @pl.when(jnp.logical_not(turned))
    def _():
        out_ref[...] = blocks.reshape(out_ref.shape).astype(BF16)


def turn(array, shape, step, direction, token=False):
    shapes = [jax.ShapeDtypeStruct(shape, BF16)]
    if token:
        shapes.append(jax.ShapeDtypeStruct((8, LANES), F32))
    return pl.pallas_call(
        functools.partial(turn_kernel, step, direction), out_shape=shapes
    )(array)


def shards(
    fields,
    level_ids,
    embed_weight,
    level_embed,
    enc_gain,
    latent_query,
    kv_weight,
    pool_out,
    attn_gain,
    qkv_weight,
    attn_proj,
    mlp_gain,
    mlp_up,
    mlp_down,
    level_mix,
    dec_gain,
    dec_weight,
):
    devices = lax.axis_size("lon")
    width = fields.shape[2]
    local_count = fields.shape[1]
    piece_cols = local_count // devices
    lat_count = devices // ROW_PARTS
    bands = lat_count // W_LAT
    cut = (W_LON // 2 // piece_cols) * lat_count
    scalars = (level_ids, level_mix.T)
    rows = (
        level_embed,
        latent_query,
        enc_gain.reshape(1, D),
        attn_gain.reshape(1, D),
        mlp_gain.reshape(1, D),
        dec_gain.reshape(1, D),
    )
    outgoing, token = turn(
        fields.reshape(local_count, width), (devices, piece_cols, width), cut, 1, token=True
    )
    early = load(token, scalars, rows, dec_weight.T, (embed_weight, kv_weight, pool_out))
    late = (qkv_weight, attn_proj, mlp_up, mlp_down)
    got = lax.all_to_all(outgoing, "lon", split_axis=0, concat_axis=0, tiled=True)
    if bands > 1:
        got = got.reshape(ROW_PARTS, lat_count, piece_cols, width)
        got = jnp.roll(got, -(W_LAT // 2), axis=1)
        got = got.reshape(ROW_PARTS, bands, W_LAT, piece_cols, width).transpose(1, 0, 2, 3, 4)
    done = forecast(bands, got.reshape(bands, ROW_PARTS * W_LAT, piece_cols, width), early, late)
    if bands > 1:
        done = done.reshape(bands, ROW_PARTS, W_LAT, piece_cols, width).transpose(1, 0, 2, 3, 4)
        done = done.reshape(ROW_PARTS, lat_count, piece_cols, width)
        done = jnp.roll(done, W_LAT // 2, axis=1)
    done = done.reshape(devices, piece_cols, width)
    home = lax.all_to_all(done, "lon", split_axis=0, concat_axis=0, tiled=True)
    (forecast_here,) = turn(home, (local_count, width), cut, -1)
    return forecast_here.reshape(fields.shape)


def solution(mesh):
    placed = (P(("groups", "lon"), None, None), P("groups")) + (P(),) * 15
    return jax.shard_map(
        shards,
        mesh=mesh,
        in_specs=placed,
        out_specs=P(("groups", "lon"), None, None),
        check_vma=False,
    )
```

profile of v0, /device:TPU:0, one launch (start us, length us, event | category | flops | bytes accessed | tf_op | source)
XLA Modules:
  0.0 40.0 jit_solution(4850715336053535113)
XLA Ops:
  0.0 1.6 %shard_map.163 = (bf16[16,2,1500]{2,1,0:T(2,128)(2,1)}, f32[8,128]{1,0:T(8,128)}) custom-call(bf16[32,1500]{1,0:T(8,128)(2,1)} %bitcast.13), custom_call_target="tpu_custom_call" | custom-call | tf_op jit(solution)/shard_map/pallas_call | solution.py:374
  1.6 7.4 %all-to-all-start = ((bf16[16,2,1500]{2,1,0:T(2,128)(2,1)}), bf16[16,2,1500]{2,1,0:T(2,128)(2,1)S(1)}, u32[]{:S(2)}, u32[]{:S(2)}) async-start(bf16[16,2,1500]{2,1,0:T(2,128)(2,1)} %get-tuple-element.30), calls=%async_computation | async-start | bytes 196608 | tf_op jit(solution)/shard_map/all_to_all | solution.py:419
  9.0 1.9 %shard_map.164 = (f32[16,512]{1,0:T(8,128)S(1)}, bf16[512,128]{1,0:T(8,128)(2,1)S(1)}, bf16[512,128]{1,0:T(8,128)(2,1)S(1)}, bf16[16,1024]{1,0:T(8,128)(2,1)S(1)...) custom-call(s32[3]{0:T(128)} %refs_0_.1, ...), custom_call_target="tpu_custom_call" | custom-call | bytes 8000000 | tf_op jit(solution)/shard_map/pallas_call | solution.py:172
  10.9 5.5 %all-to-all-done = bf16[16,2,1500]{2,1,0:T(2,128)(2,1)S(1)} async-done(((bf16[16,2,1500]{2,1,0:T(2,128)(2,1)}), bf16[16,2,1500]{2,1,0:T(2,128)(2,1)S(1)}, u32[]{:S(2)}, u32[]{:S(2)}) %all-to-all-start) | async-done | bytes 96032 | tf_op jit(solution)/shard_map/all_to_all | solution.py:419
  16.4 0.0 copy-start
  16.4 0.6 %copy-done = bf16[16,2,1500]{2,1,0:T(2,128)(2,1)} copy-done((bf16[16,2,1500]{2,1,0:T(2,128)(2,1)}, bf16[16,2,1500]{2,1,0:T(2,128)(2,1)S(1)}, u32[]{:S(2)}) %copy-start) | copy-done | bytes 96024
  17.1 9.7 %shard_map.165 = bf16[1,16,2,1500]{3,2,1,0:T(2,128)(2,1)} custom-call(f32[16,512]{1,0:T(8,128)S(1)} %get-tuple-element.19.refs_0_, bf16[512,128]{1,0:T(8,128)(2,1)S(1)} %get-tuple-element.20.refs_1_, bf16[512,128]{1,0:T(8,128)(2,1)S(1)} %get-tuple-element.21.refs_2_, bf16[16,1024]{1,0:T(8,128)(2,1)S(1)} %get-tuple-element.22.refs_3_, ...), custom_call_target="tpu_custom_call" | custom-call | tf_op jit(solution)/shard_map/pallas_call | solution.py:334
  26.8 11.6 %all_to_all.10.x_ref = bf16[16,2,1500]{2,1,0:T(2,128)(2,1)} all-to-all(bf16[16,2,1500]{2,1,0:T(2,128)(2,1)} %bitcast.12), channel_id=1, replica_groups=mesh['groups'=2,'lon'=16] {'lon'}, dimensions={0} | all-to-all | bytes 192000 | tf_op jit(solution)/shard_map/all_to_all | solution.py:430
  38.4 1.6 %shard_map.166 = bf16[32,1500]{1,0:T(8,128)(2,1)} custom-call(bf16[16,2,1500]{2,1,0:T(2,128)(2,1)} %all_to_all.10.x_ref), custom_call_target="tpu_custom_call" | custom-call | tf_op jit(solution)/shard_map/pallas_call | solution.py:374
Async XLA Ops:
  1.6 14.8 %all-to-all-start = ((bf16[16,2,1500]{2,1,0:T(2,128)(2,1)}), bf16[16,2,1500]{2,1,0:T(2,128)(2,1)S(1)}, u32[]{:S(2)}, u32[]{:S(2)}) async-start(bf16[16,2,1500]{2,1,0:T(2,128)(2,1)} %get-tuple-element.30), calls=%async_computation | async-start | bytes 196608 | tf_op jit(solution)/shard_map/all_to_all | solution.py:419
  16.4 0.6 %copy-start = (bf16[16,2,1500]{2,1,0:T(2,128)(2,1)}, bf16[16,2,1500]{2,1,0:T(2,128)(2,1)S(1)}, u32[]{:S(2)}) copy-start(bf16[16,2,1500]{2,1,0:T(2,128)(2,1)S(1)} %all-to-all-done) | copy-start | bytes 288004
where the time goes:
time: 40.4 us; the launch traced here: 40 us
  Pallas kernels  14.8 us (37%)
  blocking collectives  11.6 us (29%)
  starting transfers between devices  7.39 us (18%)
  waiting for transfers between devices  5.51 us (14%)
  local copies, waits for them, and re-layouts  0.64 us (2%)
    all_to_all x1, blocking collectives, shards(): home = lax.all_to_all(done, 'lon', split_axis=0, concat_axis=0, tiled=True)  11.6 us
    pallas_call x1, Pallas kernels, forecast(): pl.pallas_call(functools.partial(forecast_kernel, windows), grid=grid, in...  9.74 us
    all_to_all x1, starting transfers between devices, shards(): lax.all_to_all(outgoing, 'lon', split_axis=0, concat_axis=0, tiled=True)  7.39 us
    all_to_all x1, waiting for transfers between devices, shards(): lax.all_to_all(outgoing, 'lon', split_axis=0, concat_axis=0, tiled=True)  5.51 us
    pallas_call x2, Pallas kernels, turn(): pl.pallas_call(functools.partial(turn_kernel, step, direction), out_shape...  3.21 us
    pallas_call x1, Pallas kernels, load(): pl.pallas_call(load_kernel, in_specs=[far] * (len(inputs) + 1), out_specs...  1.89 us
  transfers between devices with their start and end apart: 1, of which 1 were waited for; matrix products, arithmetic and copies ran while one was open for 0% of the time, Pallas kernels for 5%

commit v1 on v0

--- a/solution.py
+++ b/solution.py
@@ -327,7 +327,10 @@
     vmem = pl.BlockSpec(memory_space=pltpu.VMEM)
     if windows == 1:
         block, grid = vmem, ()
+        result = pltpu.VMEM(arranged.shape, BF16)
+        arranged = pltpu.with_memory_space_constraint(arranged, pltpu.VMEM)
     else:
+        result = jax.ShapeDtypeStruct(arranged.shape, BF16)
         block = pl.BlockSpec((1,) + arranged.shape[1:], lambda i: (i, 0, 0, 0))
         grid = (windows,)
     early = [pltpu.with_memory_space_constraint(a, pltpu.VMEM) for a in early]
@@ -336,7 +339,7 @@
         grid=grid,
         in_specs=[vmem] * EARLY + [pl.BlockSpec(memory_space=pl.ANY)] * LATE + [block],
         out_specs=block,
-        out_shape=jax.ShapeDtypeStruct(arranged.shape, BF16),
+        out_shape=result,
         scratch_shapes=[pltpu.VMEM(a.shape, a.dtype) for a in late]
         + [
             pltpu.VMEM((LEV * PATCHES, PIN), F32),

time: 40.4 us -> 37.2 us (0.921)
  Pallas kernels: 14.8 us -> 13.3 us
  blocking collectives: 11.6 us -> 10.7 us
  local copies, waits for them, and re-layouts: 0.64 us -> 0 us
    pallas_call x1, Pallas kernels: 9.74 us -> 8.22 us  [forecast(): pl.pallas_call(functools.partial(forecast_kernel, windows), grid=grid, in...]
    all_to_all x1, blocking collectives: 11.6 us -> 10.7 us  [shards(): home = lax.all_to_all(done, 'lon', split_axis=0, concat_axis=0, tiled=True)]
    unnamed x2 -> x0, local copies, waits for them, and re-layouts: 0.64 us -> none
where the time goes in v1:
time: 37.2 us; the launch traced here: 36.9 us
  Pallas kernels  13.3 us (36%)
  blocking collectives  10.7 us (29%)
  starting transfers between devices  7.39 us (20%)
  waiting for transfers between devices  5.51 us (15%)
    all_to_all x1, blocking collectives, shards(): home = lax.all_to_all(done, 'lon', split_axis=0, concat_axis=0, tiled=True)  10.7 us
    pallas_call x1, Pallas kernels, forecast(): pl.pallas_call(functools.partial(forecast_kernel, windows), grid=grid, in...  8.22 us
    all_to_all x1, starting transfers between devices, shards(): lax.all_to_all(outgoing, 'lon', split_axis=0, concat_axis=0, tiled=True)  7.39 us
    all_to_all x1, waiting for transfers between devices, shards(): lax.all_to_all(outgoing, 'lon', split_axis=0, concat_axis=0, tiled=True)  5.51 us
    pallas_call x2, Pallas kernels, turn(): pl.pallas_call(functools.partial(turn_kernel, step, direction), out_shape...  3.21 us
    pallas_call x1, Pallas kernels, load(): pl.pallas_call(load_kernel, in_specs=[far] * (len(inputs) + 1), out_specs...  1.89 us
  transfers between devices with their start and end apart: 1, of which 1 were waited for; matrix products, arithmetic and copies ran while one was open for 0% of the time, Pallas kernels for 5%

profile of v1, /device:TPU:0, one launch (start us, length us, event | category | flops | bytes accessed | tf_op | source)
XLA Modules:
  0.0 36.9 jit_solution(649930814592471347)
XLA Ops:
  0.0 1.6 %shard_map.163 = (bf16[16,2,1500]{2,1,0:T(2,128)(2,1)}, f32[8,128]{1,0:T(8,128)}) custom-call(bf16[32,1500]{1,0:T(8,128)(2,1)} %bitcast.13), custom_call_target="tpu_custom_call" | custom-call | tf_op jit(solution)/shard_map/pallas_call | solution.py:377
  1.6 7.4 %all-to-all-start = ((bf16[16,2,1500]{2,1,0:T(2,128)(2,1)}), bf16[16,2,1500]{2,1,0:T(2,128)(2,1)S(1)}, u32[]{:S(2)}, u32[]{:S(2)}) async-start(bf16[16,2,1500]{2,1,0:T(2,128)(2,1)} %get-tuple-element.30), calls=%async_computation | async-start | bytes 196608 | tf_op jit(solution)/shard_map/all_to_all | solution.py:422
  9.0 1.9 %shard_map.164 = (f32[16,512]{1,0:T(8,128)S(1)}, bf16[512,128]{1,0:T(8,128)(2,1)S(1)}, bf16[512,128]{1,0:T(8,128)(2,1)S(1)}, bf16[16,1024]{1,0:T(8,128)(2,1)S(1)...) custom-call(s32[3]{0:T(128)} %refs_0_.1, ...), custom_call_target="tpu_custom_call" | custom-call | bytes 8000000 | tf_op jit(solution)/shard_map/pallas_call | solution.py:172
  10.9 5.5 %all-to-all-done = bf16[16,2,1500]{2,1,0:T(2,128)(2,1)S(1)} async-done(((bf16[16,2,1500]{2,1,0:T(2,128)(2,1)}), bf16[16,2,1500]{2,1,0:T(2,128)(2,1)S(1)}, u32[]{:S(2)}, u32[]{:S(2)}) %all-to-all-start) | async-done | bytes 96032 | tf_op jit(solution)/shard_map/all_to_all | solution.py:422
  16.4 8.2 %shard_map.165 = bf16[1,16,2,1500]{3,2,1,0:T(2,128)(2,1)S(1)} custom-call(f32[16,512]{1,0:T(8,128)S(1)} %get-tuple-element.19.refs_0_, bf16[512,128]{1,0:T(8,128)(2,1)S(1)} %get-tuple-element.20.refs_1_, bf16[512,128]{1,0:T(8,128)(2,1)S(1)} %get-tuple-element.21.refs_2_, bf16[16,1024]{1,0:T(8,128)(2,1)S(1)} %get-tuple-element.22.refs_3_, ...), custom_call_target="tpu_custom_call" | custom-call | tf_op jit(solution)/shard_map/pallas_call | solution.py:337
  24.7 10.7 %all_to_all.10.x_ref = bf16[16,2,1500]{2,1,0:T(2,128)(2,1)} all-to-all(bf16[16,2,1500]{2,1,0:T(2,128)(2,1)S(1)} %bitcast.11), channel_id=1, replica_groups=mesh['groups'=2,'lon'=16] {'lon'}, dimensions={0} | all-to-all | bytes 192000 | tf_op jit(solution)/shard_map/all_to_all | solution.py:433
  35.3 1.6 %shard_map.166 = bf16[32,1500]{1,0:T(8,128)(2,1)} custom-call(bf16[16,2,1500]{2,1,0:T(2,128)(2,1)} %all_to_all.10.x_ref), custom_call_target="tpu_custom_call" | custom-call | tf_op jit(solution)/shard_map/pallas_call | solution.py:377
Async XLA Ops:
  1.6 14.8 %all-to-all-start = ((bf16[16,2,1500]{2,1,0:T(2,128)(2,1)}), bf16[16,2,1500]{2,1,0:T(2,128)(2,1)S(1)}, u32[]{:S(2)}, u32[]{:S(2)}) async-start(bf16[16,2,1500]{2,1,0:T(2,128)(2,1)} %get-tuple-element.30), calls=%async_computation | async-start | bytes 196608 | tf_op jit(solution)/shard_map/all_to_all | solution.py:422

commit v2 on v1

--- a/solution.py
+++ b/solution.py
@@ -47,7 +47,7 @@
     average = jnp.mean(values, axis=-1, keepdims=True)
     centred = values - average
     spread = jnp.mean(centred * centred, axis=-1, keepdims=True)
-    return centred * lax.rsqrt(spread + norm_eps) * gain
+    return (centred * gain).astype(BF16), lax.rsqrt(spread + norm_eps)
 
 
 def iota(shape, dim):
@@ -241,6 +241,7 @@
         return entry(MIX_ROW + l * LATL + j)
 
     low = iota((1, PAIR), 1) < HEAD_DIM
+    each = jnp.full((16, PAIR), 1.0 / HEAD_DIM, BF16)
 
     arrived = x_ref[0].astype(F32).reshape(PATCHES, LEV * PIN)
     for l in range(LEV):
@@ -252,17 +253,19 @@
     for turn_index in range(STEPS):
         tokens = by_level(mm(state[...].astype(BF16), embed_ref[...]))
         tokens = jnp.concatenate([tokens[l] + embed(l) for l in range(LEV)], axis=0)
-        tokens = layer_norm(tokens, entry(GAIN_ROW)).astype(BF16)
+        tokens, factor = layer_norm(tokens, entry(GAIN_ROW))
         keyval = mm(tokens, kv_ref[...])
         keys = keyval[:, :D]
         values = by_level(keyval[:, D:])
-        mean_square = mm((keys * keys).astype(BF16), mean_ref[...])
-        scores = mm(keys.astype(BF16), query_ref[...])
-        scores = scores * lax.rsqrt(mean_square + head_eps) * HEAD_DIM ** (-0.5)
-        scores = scores[:, : LATL * HEADS]
-        parts = by_level(jnp.exp(scores))
+        mean_square = mm((keys * keys).astype(BF16), mean_ref[...])[:, : LATL * HEADS]
+        scores = mm(keys.astype(BF16), query_ref[...])[:, : LATL * HEADS]
+        scale = factor * lax.rsqrt(factor * factor * mean_square + head_eps)
+        parts = by_level(jnp.exp(scores * scale * HEAD_DIM ** (-0.5)))
         inverse = 1.0 / (parts[0] + parts[1] + parts[2])
-        weights = jnp.concatenate([part * inverse for part in parts], axis=0).astype(BF16)
+        factors = by_level(factor)
+        weights = jnp.concatenate(
+            [parts[l] * (inverse * factors[l]) for l in range(LEV)], axis=0
+        ).astype(BF16)
         wide_weights = by_level(mm(weights, spread_ref[...]))
         pooled = []
         for j in range(LATL):
@@ -276,47 +279,49 @@
             ],
             axis=0,
         )
-        normed = layer_norm(latents, entry(GAIN_ROW + 1)).astype(BF16)
+        normed, factor = layer_norm(latents, entry(GAIN_ROW + 1))
         wait(turn_index, 0)
         projected = mm(normed, qkv_ref[...])
         allowed = allowed_ref[...]
         if windows > 1:
             cut = jnp.where(pl.program_id(0) == windows - 1, 1.0, 0.0)
             allowed = 1.0 - cut * (1.0 - allowed)
-        halves = jnp.concatenate(
-            [projected[:, i * HALF : (i + 1) * HALF] for i in range(4)], axis=0
-        )
-        mean_square = mm((halves * halves).astype(BF16), ones_ref[...])
-        halves = halves * lax.rsqrt(mean_square + head_eps)
-        win_values = projected[:, 2 * D :]
+        queries = jnp.concatenate([projected[:, :HALF], projected[:, HALF:D]], axis=0)
+        mean_square = mm((queries * queries).astype(BF16), ones_ref[...])
+        twice = jnp.concatenate([factor, factor], axis=0)
+        query_scale = lax.rsqrt(twice * twice * mean_square + head_eps)
+        query_scale = query_scale * (twice * HEAD_DIM ** (-0.5))
+        win_keys = projected[:, D : 2 * D] * factor
+        win_values = projected[:, 2 * D :] * factor
         mixed = []
         for pair in range(HEADS // 2):
             half, at = pair // 2, (pair % 2) * PAIR
-            query = halves[half * TOKENS : (half + 1) * TOKENS, at : at + PAIR].astype(BF16)
-            key = halves[(2 + half) * TOKENS : (3 + half) * TOKENS, at : at + PAIR]
+            rows = slice(half * TOKENS, (half + 1) * TOKENS)
+            query = queries[rows, at : at + PAIR].astype(BF16)
+            key = win_keys[:, pair * PAIR : (pair + 1) * PAIR]
             value = win_values[:, pair * PAIR : (pair + 1) * PAIR]
-            key = jnp.concatenate(
-                [jnp.where(low, key, 0.0), jnp.where(low, 0.0, key)], axis=0
-            ).astype(BF16)
+            key = jnp.concatenate([jnp.where(low, key, 0.0), jnp.where(low, 0.0, key)], axis=0)
             value = jnp.concatenate(
                 [jnp.where(low, value, 0.0), jnp.where(low, 0.0, value)], axis=0
             ).astype(BF16)
-            weights = jnp.exp(mm_t(query, key) * HEAD_DIM ** (-0.5)) * allowed
+            key_square = mm_t(each, (key * key).astype(BF16))[:1]
+            scale = query_scale[rows, at : at + PAIR] * lax.rsqrt(key_square + head_eps)
+            weights = jnp.exp(mm_t(query, key.astype(BF16)) * scale) * allowed
             both = mm(weights.astype(BF16), jnp.concatenate([value, half_ref[...]], axis=1))
             mixed.append((both[:, :PAIR] / both[:, PAIR:]).astype(BF16))
         wait(turn_index, 1)
         attended = latents + mm(jnp.concatenate(mixed, axis=1), proj_ref[...])
-        normed = layer_norm(attended, entry(GAIN_ROW + 2)).astype(BF16)
+        normed, factor = layer_norm(attended, entry(GAIN_ROW + 2))
         wait(turn_index, 2)
-        hidden = jax.nn.gelu(mm(normed, up_ref[...])).astype(BF16)
+        hidden = jax.nn.gelu(mm(normed, up_ref[...]) * factor).astype(BF16)
         wait(turn_index, 3)
         backbone = attended + mm(hidden, down_ref[...])
         first, second = backbone[:PATCHES], backbone[PATCHES:]
         blended = jnp.concatenate(
             [mixing(l, 0) * first + mixing(l, 1) * second + embed(l) for l in range(LEV)], axis=0
         )
-        normed = layer_norm(blended, entry(GAIN_ROW + 3)).astype(BF16)
-        state[...] = (state[...] + mm(normed, dec_ref[...])).astype(BF16).astype(F32)
+        normed, factor = layer_norm(blended, entry(GAIN_ROW + 3))
+        state[...] = (state[...] + mm(normed, dec_ref[...]) * factor).astype(BF16).astype(F32)
 
     for l in range(LEV):
         wide[:, l * PIN : (l + 1) * PIN] = state[l * PATCHES : (l + 1) * PATCHES, :]

time: 37.2 us -> 36.8 us (0.989)
  Pallas kernels: 13.3 us -> 12.9 us
    pallas_call x1, Pallas kernels: 8.22 us -> 7.77 us  [forecast(): pl.pallas_call(functools.partial(forecast_kernel, windows), grid=grid, in...]
where the time goes in v2:
time: 36.8 us; the launch traced here: 36.5 us
  Pallas kernels  12.9 us (35%)
  blocking collectives  10.7 us (29%)
  starting transfers between devices  7.39 us (20%)
  waiting for transfers between devices  5.51 us (15%)
    all_to_all x1, blocking collectives, shards(): home = lax.all_to_all(done, 'lon', split_axis=0, concat_axis=0, tiled=True)  10.7 us
    pallas_call x1, Pallas kernels, forecast(): pl.pallas_call(functools.partial(forecast_kernel, windows), grid=grid, in...  7.77 us
    all_to_all x1, starting transfers between devices, shards(): lax.all_to_all(outgoing, 'lon', split_axis=0, concat_axis=0, tiled=True)  7.39 us
    all_to_all x1, waiting for transfers between devices, shards(): lax.all_to_all(outgoing, 'lon', split_axis=0, concat_axis=0, tiled=True)  5.51 us
    pallas_call x2, Pallas kernels, turn(): pl.pallas_call(functools.partial(turn_kernel, step, direction), out_shape...  3.21 us
    pallas_call x1, Pallas kernels, load(): pl.pallas_call(load_kernel, in_specs=[far] * (len(inputs) + 1), out_specs...  1.89 us
  transfers between devices with their start and end apart: 1, of which 1 were waited for; matrix products, arithmetic and copies ran while one was open for 0% of the time, Pallas kernels for 5%

profile of v2, /device:TPU:0, one launch (start us, length us, event | category | flops | bytes accessed | tf_op | source)
XLA Modules:
  0.0 36.5 jit_solution(6146067044268216541)
XLA Ops:
  0.0 1.6 %shard_map.163 = (bf16[16,2,1500]{2,1,0:T(2,128)(2,1)}, f32[8,128]{1,0:T(8,128)}) custom-call(bf16[32,1500]{1,0:T(8,128)(2,1)} %bitcast.13), custom_call_target="tpu_custom_call" | custom-call | tf_op jit(solution)/shard_map/pallas_call | solution.py:382
  1.6 7.4 %all-to-all-start = ((bf16[16,2,1500]{2,1,0:T(2,128)(2,1)}), bf16[16,2,1500]{2,1,0:T(2,128)(2,1)S(1)}, u32[]{:S(2)}, u32[]{:S(2)}) async-start(bf16[16,2,1500]{2,1,0:T(2,128)(2,1)} %get-tuple-element.30), calls=%async_computation | async-start | bytes 196608 | tf_op jit(solution)/shard_map/all_to_all | solution.py:427
  9.0 1.9 %shard_map.164 = (f32[16,512]{1,0:T(8,128)S(1)}, bf16[512,128]{1,0:T(8,128)(2,1)S(1)}, bf16[512,128]{1,0:T(8,128)(2,1)S(1)}, bf16[16,1024]{1,0:T(8,128)(2,1)S(1)...) custom-call(s32[3]{0:T(128)} %refs_0_.1, ...), custom_call_target="tpu_custom_call" | custom-call | bytes 8000000 | tf_op jit(solution)/shard_map/pallas_call | solution.py:172
  10.9 5.5 %all-to-all-done = bf16[16,2,1500]{2,1,0:T(2,128)(2,1)S(1)} async-done(((bf16[16,2,1500]{2,1,0:T(2,128)(2,1)}), bf16[16,2,1500]{2,1,0:T(2,128)(2,1)S(1)}, u32[]{:S(2)}, u32[]{:S(2)}) %all-to-all-start) | async-done | bytes 96032 | tf_op jit(solution)/shard_map/all_to_all | solution.py:427
  16.4 7.8 %shard_map.165 = bf16[1,16,2,1500]{3,2,1,0:T(2,128)(2,1)S(1)} custom-call(f32[16,512]{1,0:T(8,128)S(1)} %get-tuple-element.19.refs_0_, bf16[512,128]{1,0:T(8,128)(2,1)S(1)} %get-tuple-element.20.refs_1_, bf16[512,128]{1,0:T(8,128)(2,1)S(1)} %get-tuple-element.21.refs_2_, bf16[16,1024]{1,0:T(8,128)(2,1)S(1)} %get-tuple-element.22.refs_3_, ...), custom_call_target="tpu_custom_call" | custom-call | tf_op jit(solution)/shard_map/pallas_call | solution.py:342
  24.2 10.7 %all_to_all.10.x_ref = bf16[16,2,1500]{2,1,0:T(2,128)(2,1)} all-to-all(bf16[16,2,1500]{2,1,0:T(2,128)(2,1)S(1)} %bitcast.11), channel_id=1, replica_groups=mesh['groups'=2,'lon'=16] {'lon'}, dimensions={0} | all-to-all | bytes 192000 | tf_op jit(solution)/shard_map/all_to_all | solution.py:438
  34.9 1.6 %shard_map.166 = bf16[32,1500]{1,0:T(8,128)(2,1)} custom-call(bf16[16,2,1500]{2,1,0:T(2,128)(2,1)} %all_to_all.10.x_ref), custom_call_target="tpu_custom_call" | custom-call | tf_op jit(solution)/shard_map/pallas_call | solution.py:382
Async XLA Ops:
  1.6 14.8 %all-to-all-start = ((bf16[16,2,1500]{2,1,0:T(2,128)(2,1)}), bf16[16,2,1500]{2,1,0:T(2,128)(2,1)S(1)}, u32[]{:S(2)}, u32[]{:S(2)}) async-start(bf16[16,2,1500]{2,1,0:T(2,128)(2,1)} %get-tuple-element.30), calls=%async_computation | async-start | bytes 196608 | tf_op jit(solution)/shard_map/all_to_all | solution.py:427

commit v3 on v2

--- a/solution.py
+++ b/solution.py
@@ -1,4 +1,5 @@
 import functools
+import math
 
 import jax
 import jax.numpy as jnp
@@ -28,6 +29,10 @@
 MAIN_LIMIT = 56 * 1024 * 1024
 EMBED_ROW, MIX_ROW, LATENT_ROW, GAIN_ROW, TABLE_ROWS = 0, 3, 9, 11, 16
 
+GELU_FIRST = math.sqrt(2.0 / math.pi)
+GELU_THIRD = 0.044715 * GELU_FIRST
+SCORE_SCALE = HEAD_DIM ** (-0.5) * math.log2(math.e)
+
 norm_eps = 1e-05
 head_eps = 1e-06
 
@@ -43,11 +48,21 @@
     return lax.dot_general(a, b, (((1,), (1,)), ((), ())), preferred_element_type=F32)
 
 
-def layer_norm(values, gain):
-    average = jnp.mean(values, axis=-1, keepdims=True)
-    centred = values - average
-    spread = jnp.mean(centred * centred, axis=-1, keepdims=True)
-    return (centred * gain).astype(BF16), lax.rsqrt(spread + norm_eps)
+def layer_norm(values, gain, centred=False):
+    if not centred:
+        values = values - jnp.mean(values, axis=-1, keepdims=True)
+    spread = jnp.mean(values * values, axis=-1, keepdims=True)
+    return (values * gain).astype(BF16), lax.rsqrt(spread + norm_eps)
+
+
+def centre(rows):
+    return rows - jnp.mean(rows, axis=-1, keepdims=True)
+
+
+def gelu(values):
+    curve = values * (GELU_FIRST + GELU_THIRD * (values * values))
+    half = 0.5 * values
+    return half + half * jnp.tanh(curve)
 
 
 def iota(shape, dim):
@@ -86,6 +101,8 @@
         latent_query_ref,
         gain_refs,
         dec_rows_ref,
+        embed_rows_ref,
+        pool_rows_ref,
         arrivals,
     ) = refs
     pairs = [
@@ -98,9 +115,9 @@
         (mlp_gain_from, gain_refs.at[2]),
         (dec_gain_from, gain_refs.at[3]),
         (dec_from, dec_rows_ref),
-        (embed_from, embed_ref),
+        (embed_from, embed_rows_ref),
+        (pool_from, pool_rows_ref),
         (kv_from, kv_ref),
-        (pool_from, pool_ref),
     ]
     copies = [
         pltpu.make_async_copy(here, there, arrivals.at[i]) for i, (here, there) in enumerate(pairs)
@@ -127,7 +144,7 @@
 
     for copy in copies[:8]:
         copy.wait()
-    level_embed = level_embed_ref[...].astype(F32)
+    level_embed = centre(level_embed_ref[...].astype(F32))
     for l in range(LEV):
         level = ids_ref[l]
         row = level_embed[LEV - 1 : LEV]
@@ -138,7 +155,7 @@
             at = MIX_ROW + l * LATL + j
             table_ref[at : at + 1, :] = jnp.full((1, D), mix_ref[j, level])
     latent = latent_query_ref[...].astype(F32)
-    table_ref[LATENT_ROW : LATENT_ROW + LATL, :] = latent
+    table_ref[LATENT_ROW : LATENT_ROW + LATL, :] = centre(latent)
     for i in range(4):
         table_ref[GAIN_ROW + i : GAIN_ROW + i + 1, :] = gain_refs[i]
     row_id = iota((LANES, D), 0)
@@ -152,8 +169,11 @@
 
     copies[8].wait()
     dec_ref[...] = dec_rows_ref[...].astype(F32).T.astype(BF16)
-    for copy in copies[9:]:
-        copy.wait()
+    copies[9].wait()
+    embed_ref[...] = centre(embed_rows_ref[...].astype(F32)).astype(BF16)
+    copies[10].wait()
+    pool_ref[...] = centre(pool_rows_ref[...].astype(F32)).astype(BF16)
+    copies[11].wait()
 
 
 def load(after, scalars, rows, dec, early):
@@ -180,6 +200,8 @@
             pltpu.VMEM((LATL, D), BF16),
             pltpu.VMEM((4, 1, D), F32),
             pltpu.VMEM(dec.shape, BF16),
+            pltpu.VMEM(early[0].shape, BF16),
+            pltpu.VMEM(early[2].shape, BF16),
             pltpu.SemaphoreType.DMA((len(inputs),)),
         ],
         compiler_params=pltpu.CompilerParams(vmem_limit_bytes=LOAD_LIMIT),
@@ -202,7 +224,7 @@
         pool_ref,
     ) = refs[:EARLY]
     far, (x_ref, out_ref), refs = refs[EARLY:][:LATE], refs[EARLY + LATE :][:2], refs[EARLY + LATE + 2 :]
-    near, (state, wide, arrivals) = refs[:LATE], refs[LATE:]
+    near, (wide, arrivals) = refs[:LATE], refs[LATE:]
     qkv_ref, proj_ref, up_ref, down_ref = near
     copies = [
         pltpu.make_async_copy(far[i], near[i], arrivals.at[i]) for i in range(LATE)
@@ -244,23 +266,24 @@
     each = jnp.full((16, PAIR), 1.0 / HEAD_DIM, BF16)
 
     arrived = x_ref[0].astype(F32).reshape(PATCHES, LEV * PIN)
-    for l in range(LEV):
-        state[l * PATCHES : (l + 1) * PATCHES, :] = arrived[:, l * PIN : (l + 1) * PIN]
+    current = jnp.concatenate(
+        [arrived[:, l * PIN : (l + 1) * PIN] for l in range(LEV)], axis=0
+    )
 
     def by_level(values):
         return [values[l * PATCHES : (l + 1) * PATCHES] for l in range(LEV)]
 
     for turn_index in range(STEPS):
-        tokens = by_level(mm(state[...].astype(BF16), embed_ref[...]))
+        tokens = by_level(mm(current.astype(BF16), embed_ref[...]))
         tokens = jnp.concatenate([tokens[l] + embed(l) for l in range(LEV)], axis=0)
-        tokens, factor = layer_norm(tokens, entry(GAIN_ROW))
+        tokens, factor = layer_norm(tokens, entry(GAIN_ROW), centred=True)
         keyval = mm(tokens, kv_ref[...])
         keys = keyval[:, :D]
         values = by_level(keyval[:, D:])
         mean_square = mm((keys * keys).astype(BF16), mean_ref[...])[:, : LATL * HEADS]
         scores = mm(keys.astype(BF16), query_ref[...])[:, : LATL * HEADS]
         scale = factor * lax.rsqrt(factor * factor * mean_square + head_eps)
-        parts = by_level(jnp.exp(scores * scale * HEAD_DIM ** (-0.5)))
+        parts = by_level(jnp.exp2(scores * (scale * SCORE_SCALE)))
         inverse = 1.0 / (parts[0] + parts[1] + parts[2])
         factors = by_level(factor)
         weights = jnp.concatenate(
@@ -279,7 +302,7 @@
             ],
             axis=0,
         )
-        normed, factor = layer_norm(latents, entry(GAIN_ROW + 1))
+        normed, factor = layer_norm(latents, entry(GAIN_ROW + 1), centred=True)
         wait(turn_index, 0)
         projected = mm(normed, qkv_ref[...])
         allowed = allowed_ref[...]
@@ -290,7 +313,7 @@
         mean_square = mm((queries * queries).astype(BF16), ones_ref[...])
         twice = jnp.concatenate([factor, factor], axis=0)
         query_scale = lax.rsqrt(twice * twice * mean_square + head_eps)
-        query_scale = query_scale * (twice * HEAD_DIM ** (-0.5))
+        query_scale = query_scale * (twice * SCORE_SCALE)
         win_keys = projected[:, D : 2 * D] * factor
         win_values = projected[:, 2 * D :] * factor
         mixed = []
@@ -306,14 +329,14 @@
             ).astype(BF16)
             key_square = mm_t(each, (key * key).astype(BF16))[:1]
             scale = query_scale[rows, at : at + PAIR] * lax.rsqrt(key_square + head_eps)
-            weights = jnp.exp(mm_t(query, key.astype(BF16)) * scale) * allowed
+            weights = jnp.exp2(mm_t(query, key.astype(BF16)) * scale) * allowed
             both = mm(weights.astype(BF16), jnp.concatenate([value, half_ref[...]], axis=1))
             mixed.append((both[:, :PAIR] / both[:, PAIR:]).astype(BF16))
         wait(turn_index, 1)
         attended = latents + mm(jnp.concatenate(mixed, axis=1), proj_ref[...])
         normed, factor = layer_norm(attended, entry(GAIN_ROW + 2))
         wait(turn_index, 2)
-        hidden = jax.nn.gelu(mm(normed, up_ref[...]) * factor).astype(BF16)
+        hidden = gelu(mm(normed, up_ref[...]) * factor).astype(BF16)
         wait(turn_index, 3)
         backbone = attended + mm(hidden, down_ref[...])
         first, second = backbone[:PATCHES], backbone[PATCHES:]
@@ -321,10 +344,10 @@
             [mixing(l, 0) * first + mixing(l, 1) * second + embed(l) for l in range(LEV)], axis=0
         )
         normed, factor = layer_norm(blended, entry(GAIN_ROW + 3))
-        state[...] = (state[...] + mm(normed, dec_ref[...]) * factor).astype(BF16).astype(F32)
+        current = (current + mm(normed, dec_ref[...]) * factor).astype(BF16).astype(F32)
 
     for l in range(LEV):
-        wide[:, l * PIN : (l + 1) * PIN] = state[l * PATCHES : (l + 1) * PATCHES, :]
+        wide[:, l * PIN : (l + 1) * PIN] = current[l * PATCHES : (l + 1) * PATCHES]
     out_ref[0] = wide[...].reshape(out_ref.shape[1:]).astype(BF16)
 
 
@@ -347,7 +370,6 @@
         out_shape=result,
         scratch_shapes=[pltpu.VMEM(a.shape, a.dtype) for a in late]
         + [
-            pltpu.VMEM((LEV * PATCHES, PIN), F32),
             pltpu.VMEM((PATCHES, LEV * PIN), F32),
             pltpu.SemaphoreType.DMA((LATE,)),
         ],
@@ -356,23 +378,18 @@
 
 
 def turn_kernel(step, direction, x_ref, out_ref, *token_ref):
-    count = x_ref.shape[0] if len(x_ref.shape) == 3 else out_ref.shape[0]
     for ref in token_ref:
         ref[...] = jnp.zeros_like(ref)
-    turned = lax.axis_index("lon") < step
-    blocks = x_ref[...].astype(F32).reshape(count, 2, LEV * PIN)
-
-    @pl.when(turned)
-    def _():
-        if direction > 0:
-            moved = jnp.concatenate([blocks[1:], blocks[:1]], axis=0)
-        else:
-            moved = jnp.concatenate([blocks[-1:], blocks[:-1]], axis=0)
-        out_ref[...] = moved.reshape(out_ref.shape).astype(BF16)
-
-    @pl.when(jnp.logical_not(turned))
-    def _():
-        out_ref[...] = blocks.reshape(out_ref.shape).astype(BF16)
+    shift = jnp.where(lax.axis_index("lon") < step, 1, 0)
+    if direction > 0:
+        count = out_ref.shape[0]
+        blocks = x_ref[...].astype(F32).reshape(out_ref.shape)
+        for i in range(count):
+            out_ref[lax.rem(i + count - shift, count)] = blocks[i].astype(BF16)
+    else:
+        count = x_ref.shape[0]
+        blocks = [x_ref[lax.rem(i + count - shift, count)].astype(F32) for i in range(count)]
+        out_ref[...] = jnp.stack(blocks).reshape(out_ref.shape).astype(BF16)
 
 
 def turn(array, shape, step, direction, token=False):

time: 36.8 us -> 36.6 us (level)
  no operation moved by 1% of the time
where the time goes in v3:
time: 36.6 us; the launch traced here: 36.3 us
  Pallas kernels  12.7 us (35%)
  blocking collectives  10.7 us (29%)
  starting transfers between devices  7.39 us (20%)
  waiting for transfers between devices  5.49 us (15%)
    all_to_all x1, blocking collectives, shards(): home = lax.all_to_all(done, 'lon', split_axis=0, concat_axis=0, tiled=True)  10.7 us
    pallas_call x1, Pallas kernels, forecast(): pl.pallas_call(functools.partial(forecast_kernel, windows), grid=grid, in...  7.62 us
    all_to_all x1, starting transfers between devices, shards(): lax.all_to_all(outgoing, 'lon', split_axis=0, concat_axis=0, tiled=True)  7.39 us
    all_to_all x1, waiting for transfers between devices, shards(): lax.all_to_all(outgoing, 'lon', split_axis=0, concat_axis=0, tiled=True)  5.49 us
    pallas_call x2, Pallas kernels, turn(): pl.pallas_call(functools.partial(turn_kernel, step, direction), out_shape...  3.21 us
    pallas_call x1, Pallas kernels, load(): pl.pallas_call(load_kernel, in_specs=[far] * (len(inputs) + 1), out_specs...  1.91 us
  transfers between devices with their start and end apart: 1, of which 1 were waited for; matrix products, arithmetic and copies ran while one was open for 0% of the time, Pallas kernels for 5%

profile of v3, /device:TPU:0, one launch (start us, length us, event | category | flops | bytes accessed | tf_op | source)
XLA Modules:
  0.0 36.3 jit_solution(17255587483435136518)
XLA Ops:
  0.0 1.6 %shard_map.163 = (bf16[16,2,1500]{2,1,0:T(2,128)(2,1)}, f32[8,128]{1,0:T(8,128)}) custom-call(bf16[32,1500]{1,0:T(8,128)(2,1)} %bitcast.13), custom_call_target="tpu_custom_call" | custom-call | tf_op jit(solution)/shard_map/pallas_call | solution.py:399
  1.6 7.4 %all-to-all-start = ((bf16[16,2,1500]{2,1,0:T(2,128)(2,1)}), bf16[16,2,1500]{2,1,0:T(2,128)(2,1)S(1)}, u32[]{:S(2)}, u32[]{:S(2)}) async-start(bf16[16,2,1500]{2,1,0:T(2,128)(2,1)} %get-tuple-element.30), calls=%async_computation | async-start | bytes 196608 | tf_op jit(solution)/shard_map/all_to_all | solution.py:444
  9.0 1.9 %shard_map.164 = (f32[16,512]{1,0:T(8,128)S(1)}, bf16[512,128]{1,0:T(8,128)(2,1)S(1)}, bf16[512,128]{1,0:T(8,128)(2,1)S(1)}, bf16[16,1024]{1,0:T(8,128)(2,1)S(1)...) custom-call(s32[3]{0:T(128)} %refs_0_.1, ...), custom_call_target="tpu_custom_call" | custom-call | bytes 8000000 | tf_op jit(solution)/shard_map/pallas_call | solution.py:192
  11.0 5.5 %all-to-all-done = bf16[16,2,1500]{2,1,0:T(2,128)(2,1)S(1)} async-done(((bf16[16,2,1500]{2,1,0:T(2,128)(2,1)}), bf16[16,2,1500]{2,1,0:T(2,128)(2,1)S(1)}, u32[]{:S(2)}, u32[]{:S(2)}) %all-to-all-start) | async-done | bytes 96032 | tf_op jit(solution)/shard_map/all_to_all | solution.py:444
  16.4 7.6 %shard_map.165 = bf16[1,16,2,1500]{3,2,1,0:T(2,128)(2,1)S(1)} custom-call(f32[16,512]{1,0:T(8,128)S(1)} %get-tuple-element.19.refs_0_, bf16[512,128]{1,0:T(8,128)(2,1)S(1)} %get-tuple-element.20.refs_1_, bf16[512,128]{1,0:T(8,128)(2,1)S(1)} %get-tuple-element.21.refs_2_, bf16[16,1024]{1,0:T(8,128)(2,1)S(1)} %get-tuple-element.22.refs_3_, ...), custom_call_target="tpu_custom_call" | custom-call | tf_op jit(solution)/shard_map/pallas_call | solution.py:365
  24.1 10.7 %all_to_all.10.x_ref = bf16[16,2,1500]{2,1,0:T(2,128)(2,1)} all-to-all(bf16[16,2,1500]{2,1,0:T(2,128)(2,1)S(1)} %bitcast.11), channel_id=1, replica_groups=mesh['groups'=2,'lon'=16] {'lon'}, dimensions={0} | all-to-all | bytes 192000 | tf_op jit(solution)/shard_map/all_to_all | solution.py:455
  34.7 1.6 %shard_map.166 = bf16[32,1500]{1,0:T(8,128)(2,1)} custom-call(bf16[16,2,1500]{2,1,0:T(2,128)(2,1)} %all_to_all.10.x_ref), custom_call_target="tpu_custom_call" | custom-call | tf_op jit(solution)/shard_map/pallas_call | solution.py:399
Async XLA Ops:
  1.6 14.8 %all-to-all-start = ((bf16[16,2,1500]{2,1,0:T(2,128)(2,1)}), bf16[16,2,1500]{2,1,0:T(2,128)(2,1)S(1)}, u32[]{:S(2)}, u32[]{:S(2)}) async-start(bf16[16,2,1500]{2,1,0:T(2,128)(2,1)} %get-tuple-element.30), calls=%async_computation | async-start | bytes 196608 | tf_op jit(solution)/shard_map/all_to_all | solution.py:444

commit v4 on v3

--- a/solution.py
+++ b/solution.py
@@ -24,6 +24,8 @@
 HALF = D // 2
 PAIR = 2 * HEAD_DIM
 EARLY, LATE = 11, 4
+PARTS = 4
+PART = MLP // PARTS
 LANES = 128
 LOAD_LIMIT = 56 * 1024 * 1024
 MAIN_LIMIT = 56 * 1024 * 1024
@@ -226,8 +228,14 @@
     far, (x_ref, out_ref), refs = refs[EARLY:][:LATE], refs[EARLY + LATE :][:2], refs[EARLY + LATE + 2 :]
     near, (wide, arrivals) = refs[:LATE], refs[LATE:]
     qkv_ref, proj_ref, up_ref, down_ref = near
+    moves = [(far[0], qkv_ref), (far[1], proj_ref)]
+    for part in range(PARTS):
+        units = pl.ds(part * PART, PART)
+        moves.append((far[2].at[:, units], up_ref.at[:, units]))
+        moves.append((far[3].at[units], down_ref.at[units]))
     copies = [
-        pltpu.make_async_copy(far[i], near[i], arrivals.at[i]) for i in range(LATE)
+        pltpu.make_async_copy(here, there, arrivals.at[i])
+        for i, (here, there) in enumerate(moves)
     ]
 
     def in_first_window(action):
@@ -251,7 +259,7 @@
         if turn_index == 0:
             in_first_window(action)
 
-    start(0, 1, 2, 3)
+    start(*range(len(copies)))
 
     def entry(at):
         return table_ref[at : at + 1, :]
@@ -265,7 +273,7 @@
     low = iota((1, PAIR), 1) < HEAD_DIM
     each = jnp.full((16, PAIR), 1.0 / HEAD_DIM, BF16)
 
-    arrived = x_ref[0].astype(F32).reshape(PATCHES, LEV * PIN)
+    arrived = x_ref[0].reshape(PATCHES, LEV * PIN).astype(F32)
     current = jnp.concatenate(
         [arrived[:, l * PIN : (l + 1) * PIN] for l in range(LEV)], axis=0
     )
@@ -335,10 +343,13 @@
         wait(turn_index, 1)
         attended = latents + mm(jnp.concatenate(mixed, axis=1), proj_ref[...])
         normed, factor = layer_norm(attended, entry(GAIN_ROW + 2))
-        wait(turn_index, 2)
-        hidden = gelu(mm(normed, up_ref[...]) * factor).astype(BF16)
-        wait(turn_index, 3)
-        backbone = attended + mm(hidden, down_ref[...])
+        backbone = attended
+        for part in range(PARTS):
+            units = slice(part * PART, (part + 1) * PART)
+            wait(turn_index, 2 + 2 * part)
+            hidden = gelu(mm(normed, up_ref[:, units]) * factor).astype(BF16)
+            wait(turn_index, 3 + 2 * part)
+            backbone = backbone + mm(hidden, down_ref[units, :])
         first, second = backbone[:PATCHES], backbone[PATCHES:]
         blended = jnp.concatenate(
             [mixing(l, 0) * first + mixing(l, 1) * second + embed(l) for l in range(LEV)], axis=0
@@ -348,7 +359,7 @@
 
     for l in range(LEV):
         wide[:, l * PIN : (l + 1) * PIN] = current[l * PATCHES : (l + 1) * PATCHES]
-    out_ref[0] = wide[...].reshape(out_ref.shape[1:]).astype(BF16)
+    out_ref[0] = wide[...].astype(BF16).reshape(out_ref.shape[1:])
 
 
 def forecast(windows, arranged, early, late):
@@ -371,7 +382,7 @@
         scratch_shapes=[pltpu.VMEM(a.shape, a.dtype) for a in late]
         + [
             pltpu.VMEM((PATCHES, LEV * PIN), F32),
-            pltpu.SemaphoreType.DMA((LATE,)),
+            pltpu.SemaphoreType.DMA((2 + 2 * PARTS,)),
         ],
         compiler_params=pltpu.CompilerParams(vmem_limit_bytes=MAIN_LIMIT),
     )(*early, *late, arranged)
@@ -383,13 +394,13 @@
     shift = jnp.where(lax.axis_index("lon") < step, 1, 0)
     if direction > 0:
         count = out_ref.shape[0]
-        blocks = x_ref[...].astype(F32).reshape(out_ref.shape)
+        blocks = x_ref[...].reshape(out_ref.shape)
         for i in range(count):
-            out_ref[lax.rem(i + count - shift, count)] = blocks[i].astype(BF16)
+            out_ref[lax.rem(i + count - shift, count)] = blocks[i]
     else:
         count = x_ref.shape[0]
-        blocks = [x_ref[lax.rem(i + count - shift, count)].astype(F32) for i in range(count)]
-        out_ref[...] = jnp.stack(blocks).reshape(out_ref.shape).astype(BF16)
+        blocks = [x_ref[lax.rem(i + count - shift, count)] for i in range(count)]
+        out_ref[...] = jnp.stack(blocks).reshape(out_ref.shape)
 
 
 def turn(array, shape, step, direction, token=False):

time: 36.6 us -> 37.4 us (1.022)
  Pallas kernels: 12.7 us -> 13.5 us
    pallas_call x1, Pallas kernels: 7.62 us -> 8.5 us  [forecast(): pl.pallas_call(functools.partial(forecast_kernel, windows), grid=grid, in...]
where the time goes in v4:
time: 37.4 us; the launch traced here: 37.1 us
  Pallas kernels  13.5 us (36%)
  blocking collectives  10.7 us (29%)
  starting transfers between devices  7.39 us (20%)
  waiting for transfers between devices  5.49 us (15%)
    all_to_all x1, blocking collectives, shards(): home = lax.all_to_all(done, 'lon', split_axis=0, concat_axis=0, tiled=True)  10.7 us
    pallas_call x1, Pallas kernels, forecast(): pl.pallas_call(functools.partial(forecast_kernel, windows), grid=grid, in...  8.5 us
    all_to_all x1, starting transfers between devices, shards(): lax.all_to_all(outgoing, 'lon', split_axis=0, concat_axis=0, tiled=True)  7.39 us
    all_to_all x1, waiting for transfers between devices, shards(): lax.all_to_all(outgoing, 'lon', split_axis=0, concat_axis=0, tiled=True)  5.49 us
    pallas_call x2, Pallas kernels, turn(): pl.pallas_call(functools.partial(turn_kernel, step, direction), out_shape...  3.13 us
    pallas_call x1, Pallas kernels, load(): pl.pallas_call(load_kernel, in_specs=[far] * (len(inputs) + 1), out_specs...  1.91 us
  transfers between devices with their start and end apart: 1, of which 1 were waited for; matrix products, arithmetic and copies ran while one was open for 0% of the time, Pallas kernels for 5%

profile of v4, /device:TPU:0, one launch (start us, length us, event | category | flops | bytes accessed | tf_op | source)
XLA Modules:
  0.0 37.1 jit_solution(4915480437224295165)
XLA Ops:
  0.0 1.6 %shard_map.163 = (bf16[16,2,1500]{2,1,0:T(2,128)(2,1)}, f32[8,128]{1,0:T(8,128)}) custom-call(bf16[32,1500]{1,0:T(8,128)(2,1)} %bitcast.13), custom_call_target="tpu_custom_call" | custom-call | tf_op jit(solution)/shard_map/pallas_call | solution.py:410
  1.6 7.4 %all-to-all-start = ((bf16[16,2,1500]{2,1,0:T(2,128)(2,1)}), bf16[16,2,1500]{2,1,0:T(2,128)(2,1)S(1)}, u32[]{:S(2)}, u32[]{:S(2)}) async-start(bf16[16,2,1500]{2,1,0:T(2,128)(2,1)} %get-tuple-element.30), calls=%async_computation | async-start | bytes 196608 | tf_op jit(solution)/shard_map/all_to_all | solution.py:455
  9.0 1.9 %shard_map.164 = (f32[16,512]{1,0:T(8,128)S(1)}, bf16[512,128]{1,0:T(8,128)(2,1)S(1)}, bf16[512,128]{1,0:T(8,128)(2,1)S(1)}, bf16[16,1024]{1,0:T(8,128)(2,1)S(1)...) custom-call(s32[3]{0:T(128)} %refs_0_.1, ...), custom_call_target="tpu_custom_call" | custom-call | bytes 8000000 | tf_op jit(solution)/shard_map/pallas_call | solution.py:194
  10.9 5.5 %all-to-all-done = bf16[16,2,1500]{2,1,0:T(2,128)(2,1)S(1)} async-done(((bf16[16,2,1500]{2,1,0:T(2,128)(2,1)}), bf16[16,2,1500]{2,1,0:T(2,128)(2,1)S(1)}, u32[]{:S(2)}, u32[]{:S(2)}) %all-to-all-start) | async-done | bytes 96032 | tf_op jit(solution)/shard_map/all_to_all | solution.py:455
  16.4 8.5 %shard_map.165 = bf16[1,16,2,1500]{3,2,1,0:T(2,128)(2,1)S(1)} custom-call(f32[16,512]{1,0:T(8,128)S(1)} %get-tuple-element.19.refs_0_, bf16[512,128]{1,0:T(8,128)(2,1)S(1)} %get-tuple-element.20.refs_1_, bf16[512,128]{1,0:T(8,128)(2,1)S(1)} %get-tuple-element.21.refs_2_, bf16[16,1024]{1,0:T(8,128)(2,1)S(1)} %get-tuple-element.22.refs_3_, ...), custom_call_target="tpu_custom_call" | custom-call | tf_op jit(solution)/shard_map/pallas_call | solution.py:376
  24.9 10.7 %all_to_all.10.x_ref = bf16[16,2,1500]{2,1,0:T(2,128)(2,1)} all-to-all(bf16[16,2,1500]{2,1,0:T(2,128)(2,1)S(1)} %bitcast.11), channel_id=1, replica_groups=mesh['groups'=2,'lon'=16] {'lon'}, dimensions={0} | all-to-all | bytes 192000 | tf_op jit(solution)/shard_map/all_to_all | solution.py:466
  35.5 1.6 %shard_map.166 = bf16[32,1500]{1,0:T(8,128)(2,1)} custom-call(bf16[16,2,1500]{2,1,0:T(2,128)(2,1)} %all_to_all.10.x_ref), custom_call_target="tpu_custom_call" | custom-call | tf_op jit(solution)/shard_map/pallas_call | solution.py:410
Async XLA Ops:
  1.6 14.8 %all-to-all-start = ((bf16[16,2,1500]{2,1,0:T(2,128)(2,1)}), bf16[16,2,1500]{2,1,0:T(2,128)(2,1)S(1)}, u32[]{:S(2)}, u32[]{:S(2)}) async-start(bf16[16,2,1500]{2,1,0:T(2,128)(2,1)} %get-tuple-element.30), calls=%async_computation | async-start | bytes 196608 | tf_op jit(solution)/shard_map/all_to_all | solution.py:455

commit v5 on v3

--- a/solution.py
+++ b/solution.py
@@ -265,7 +265,7 @@
     low = iota((1, PAIR), 1) < HEAD_DIM
     each = jnp.full((16, PAIR), 1.0 / HEAD_DIM, BF16)
 
-    arrived = x_ref[0].astype(F32).reshape(PATCHES, LEV * PIN)
+    arrived = x_ref[0].reshape(PATCHES, LEV * PIN).astype(F32)
     current = jnp.concatenate(
         [arrived[:, l * PIN : (l + 1) * PIN] for l in range(LEV)], axis=0
     )
@@ -303,7 +303,7 @@
             axis=0,
         )
         normed, factor = layer_norm(latents, entry(GAIN_ROW + 1), centred=True)
-        wait(turn_index, 0)
+        wait(turn_index, 0, 1)
         projected = mm(normed, qkv_ref[...])
         allowed = allowed_ref[...]
         if windows > 1:
@@ -332,12 +332,10 @@
             weights = jnp.exp2(mm_t(query, key.astype(BF16)) * scale) * allowed
             both = mm(weights.astype(BF16), jnp.concatenate([value, half_ref[...]], axis=1))
             mixed.append((both[:, :PAIR] / both[:, PAIR:]).astype(BF16))
-        wait(turn_index, 1)
         attended = latents + mm(jnp.concatenate(mixed, axis=1), proj_ref[...])
         normed, factor = layer_norm(attended, entry(GAIN_ROW + 2))
-        wait(turn_index, 2)
+        wait(turn_index, 2, 3)
         hidden = gelu(mm(normed, up_ref[...]) * factor).astype(BF16)
-        wait(turn_index, 3)
         backbone = attended + mm(hidden, down_ref[...])
         first, second = backbone[:PATCHES], backbone[PATCHES:]
         blended = jnp.concatenate(
@@ -348,7 +346,7 @@
 
     for l in range(LEV):
         wide[:, l * PIN : (l + 1) * PIN] = current[l * PATCHES : (l + 1) * PATCHES]
-    out_ref[0] = wide[...].reshape(out_ref.shape[1:]).astype(BF16)
+    out_ref[0] = wide[...].astype(BF16).reshape(out_ref.shape[1:])
 
 
 def forecast(windows, arranged, early, late):
@@ -383,13 +381,13 @@
     shift = jnp.where(lax.axis_index("lon") < step, 1, 0)
     if direction > 0:
         count = out_ref.shape[0]
-        blocks = x_ref[...].astype(F32).reshape(out_ref.shape)
+        blocks = x_ref[...].reshape(out_ref.shape)
         for i in range(count):
-            out_ref[lax.rem(i + count - shift, count)] = blocks[i].astype(BF16)
+            out_ref[lax.rem(i + count - shift, count)] = blocks[i]
     else:
         count = x_ref.shape[0]
-        blocks = [x_ref[lax.rem(i + count - shift, count)].astype(F32) for i in range(count)]
-        out_ref[...] = jnp.stack(blocks).reshape(out_ref.shape).astype(BF16)
+        blocks = [x_ref[lax.rem(i + count - shift, count)] for i in range(count)]
+        out_ref[...] = jnp.stack(blocks).reshape(out_ref.shape)
 
 
 def turn(array, shape, step, direction, token=False):

time: 36.6 us -> 36.3 us (level)
  no operation moved by 1% of the time
where the time goes in v5:
time: 36.3 us; the launch traced here: 36 us
  Pallas kernels  12.5 us (34%)
  blocking collectives  10.7 us (29%)
  starting transfers between devices  7.39 us (20%)
  waiting for transfers between devices  5.49 us (15%)
    all_to_all x1, blocking collectives, shards(): home = lax.all_to_all(done, 'lon', split_axis=0, concat_axis=0, tiled=True)  10.7 us
    pallas_call x1, Pallas kernels, forecast(): pl.pallas_call(functools.partial(forecast_kernel, windows), grid=grid, in...  7.42 us
    all_to_all x1, starting transfers between devices, shards(): lax.all_to_all(outgoing, 'lon', split_axis=0, concat_axis=0, tiled=True)  7.39 us
    all_to_all x1, waiting for transfers between devices, shards(): lax.all_to_all(outgoing, 'lon', split_axis=0, concat_axis=0, tiled=True)  5.49 us
    pallas_call x2, Pallas kernels, turn(): pl.pallas_call(functools.partial(turn_kernel, step, direction), out_shape...  3.13 us
    pallas_call x1, Pallas kernels, load(): pl.pallas_call(load_kernel, in_specs=[far] * (len(inputs) + 1), out_specs...  1.91 us
  transfers between devices with their start and end apart: 1, of which 1 were waited for; matrix products, arithmetic and copies ran while one was open for 0% of the time, Pallas kernels for 5%

profile of v5, /device:TPU:0, one launch (start us, length us, event | category | flops | bytes accessed | tf_op | source)
XLA Modules:
  0.0 36.0 jit_solution(17492421868699146503)
XLA Ops:
  0.0 1.6 %shard_map.163 = (bf16[16,2,1500]{2,1,0:T(2,128)(2,1)}, f32[8,128]{1,0:T(8,128)}) custom-call(bf16[32,1500]{1,0:T(8,128)(2,1)} %bitcast.13), custom_call_target="tpu_custom_call" | custom-call | tf_op jit(solution)/shard_map/pallas_call | solution.py:397
  1.6 7.4 %all-to-all-start = ((bf16[16,2,1500]{2,1,0:T(2,128)(2,1)}), bf16[16,2,1500]{2,1,0:T(2,128)(2,1)S(1)}, u32[]{:S(2)}, u32[]{:S(2)}) async-start(bf16[16,2,1500]{2,1,0:T(2,128)(2,1)} %get-tuple-element.30), calls=%async_computation | async-start | bytes 196608 | tf_op jit(solution)/shard_map/all_to_all | solution.py:442
  9.0 1.9 %shard_map.164 = (f32[16,512]{1,0:T(8,128)S(1)}, bf16[512,128]{1,0:T(8,128)(2,1)S(1)}, bf16[512,128]{1,0:T(8,128)(2,1)S(1)}, bf16[16,1024]{1,0:T(8,128)(2,1)S(1)...) custom-call(s32[3]{0:T(128)} %refs_0_.1, ...), custom_call_target="tpu_custom_call" | custom-call | bytes 8000000 | tf_op jit(solution)/shard_map/pallas_call | solution.py:192
  10.9 5.5 %all-to-all-done = bf16[16,2,1500]{2,1,0:T(2,128)(2,1)S(1)} async-done(((bf16[16,2,1500]{2,1,0:T(2,128)(2,1)}), bf16[16,2,1500]{2,1,0:T(2,128)(2,1)S(1)}, u32[]{:S(2)}, u32[]{:S(2)}) %all-to-all-start) | async-done | bytes 96032 | tf_op jit(solution)/shard_map/all_to_all | solution.py:442
  16.4 7.4 %shard_map.165 = bf16[1,16,2,1500]{3,2,1,0:T(2,128)(2,1)S(1)} custom-call(f32[16,512]{1,0:T(8,128)S(1)} %get-tuple-element.19.refs_0_, bf16[512,128]{1,0:T(8,128)(2,1)S(1)} %get-tuple-element.20.refs_1_, bf16[512,128]{1,0:T(8,128)(2,1)S(1)} %get-tuple-element.21.refs_2_, bf16[16,1024]{1,0:T(8,128)(2,1)S(1)} %get-tuple-element.22.refs_3_, ...), custom_call_target="tpu_custom_call" | custom-call | tf_op jit(solution)/shard_map/pallas_call | solution.py:363
  23.8 10.7 %all_to_all.10.x_ref = bf16[16,2,1500]{2,1,0:T(2,128)(2,1)} all-to-all(bf16[16,2,1500]{2,1,0:T(2,128)(2,1)S(1)} %bitcast.11), channel_id=1, replica_groups=mesh['groups'=2,'lon'=16] {'lon'}, dimensions={0} | all-to-all | bytes 192000 | tf_op jit(solution)/shard_map/all_to_all | solution.py:453
  34.5 1.6 %shard_map.166 = bf16[32,1500]{1,0:T(8,128)(2,1)} custom-call(bf16[16,2,1500]{2,1,0:T(2,128)(2,1)} %all_to_all.10.x_ref), custom_call_target="tpu_custom_call" | custom-call | tf_op jit(solution)/shard_map/pallas_call | solution.py:397
Async XLA Ops:
  1.6 14.8 %all-to-all-start = ((bf16[16,2,1500]{2,1,0:T(2,128)(2,1)}), bf16[16,2,1500]{2,1,0:T(2,128)(2,1)S(1)}, u32[]{:S(2)}, u32[]{:S(2)}) async-start(bf16[16,2,1500]{2,1,0:T(2,128)(2,1)} %get-tuple-element.30), calls=%async_computation | async-start | bytes 196608 | tf_op jit(solution)/shard_map/all_to_all | solution.py:442

commit v6 on v5

--- a/solution.py
+++ b/solution.py
@@ -23,7 +23,7 @@
 TOKENS = PATCHES * LATL
 HALF = D // 2
 PAIR = 2 * HEAD_DIM
-EARLY, LATE = 11, 4
+EARLY, LATE = 10, 4
 LANES = 128
 LOAD_LIMIT = 56 * 1024 * 1024
 MAIN_LIMIT = 56 * 1024 * 1024
@@ -48,11 +48,8 @@
     return lax.dot_general(a, b, (((1,), (1,)), ((), ())), preferred_element_type=F32)
 
 
-def layer_norm(values, gain, centred=False):
-    if not centred:
-        values = values - jnp.mean(values, axis=-1, keepdims=True)
-    spread = jnp.mean(values * values, axis=-1, keepdims=True)
-    return (values * gain).astype(BF16), lax.rsqrt(spread + norm_eps)
+def row_factor(centred):
+    return lax.rsqrt(jnp.mean(centred * centred, axis=-1, keepdims=True) + norm_eps)
 
 
 def centre(rows):
@@ -89,7 +86,6 @@
         mean_ref,
         spread_ref,
         ones_ref,
-        half_ref,
         allowed_ref,
         dec_ref,
         embed_ref,
@@ -135,9 +131,6 @@
     ones_ref[...] = jnp.where(
         iota((HALF, HALF), 0) // HEAD_DIM == iota((HALF, HALF), 1) // HEAD_DIM, 1.0 / HEAD_DIM, 0.0
     ).astype(BF16)
-    half_ref[...] = jnp.where(
-        (iota((PAIR, PAIR), 0) < HEAD_DIM) == (iota((PAIR, PAIR), 1) < HEAD_DIM), 1.0, 0.0
-    ).astype(BF16)
     row_bit = (iota((TOKENS, PAIR), 0) // 4) % 2
     lane_bit = (iota((TOKENS, PAIR), 1) // 4) % 2
     allowed_ref[...] = jnp.where(row_bit == lane_bit, 1.0, 0.0)
@@ -184,7 +177,6 @@
         pltpu.VMEM((D, LANES), BF16),
         pltpu.VMEM((LATL * HEADS, LATL * D), BF16),
         pltpu.VMEM((HALF, HALF), BF16),
-        pltpu.VMEM((PAIR, PAIR), BF16),
         pltpu.VMEM((TOKENS, PAIR), F32),
         pltpu.VMEM(dec.shape[::-1], BF16),
     ] + [pltpu.VMEM(a.shape, a.dtype) for a in early]
@@ -216,7 +208,6 @@
         mean_ref,
         spread_ref,
         ones_ref,
-        half_ref,
         allowed_ref,
         dec_ref,
         embed_ref,
@@ -262,8 +253,8 @@
     def mixing(l, j):
         return entry(MIX_ROW + l * LATL + j)
 
-    low = iota((1, PAIR), 1) < HEAD_DIM
-    each = jnp.full((16, PAIR), 1.0 / HEAD_DIM, BF16)
+    half_head = iota((1, HALF), 1) // HEAD_DIM
+    each = jnp.full((16, HALF), 1.0 / HEAD_DIM, BF16)
 
     arrived = x_ref[0].reshape(PATCHES, LEV * PIN).astype(F32)
     current = jnp.concatenate(
@@ -276,12 +267,12 @@
     for turn_index in range(STEPS):
         tokens = by_level(mm(current.astype(BF16), embed_ref[...]))
         tokens = jnp.concatenate([tokens[l] + embed(l) for l in range(LEV)], axis=0)
-        tokens, factor = layer_norm(tokens, entry(GAIN_ROW), centred=True)
-        keyval = mm(tokens, kv_ref[...])
+        keyval = mm((tokens * entry(GAIN_ROW)).astype(BF16), kv_ref[...])
+        factor = row_factor(tokens)
         keys = keyval[:, :D]
         values = by_level(keyval[:, D:])
+        scores = mm(keys.astype(BF16), query_ref[...])[:, : LATL * HEADS]
         mean_square = mm((keys * keys).astype(BF16), mean_ref[...])[:, : LATL * HEADS]
-        scores = mm(keys.astype(BF16), query_ref[...])[:, : LATL * HEADS]
         scale = factor * lax.rsqrt(factor * factor * mean_square + head_eps)
         parts = by_level(jnp.exp2(scores * (scale * SCORE_SCALE)))
         inverse = 1.0 / (parts[0] + parts[1] + parts[2])
@@ -302,47 +293,57 @@
             ],
             axis=0,
         )
-        normed, factor = layer_norm(latents, entry(GAIN_ROW + 1), centred=True)
         wait(turn_index, 0, 1)
-        projected = mm(normed, qkv_ref[...])
+        projected = mm((latents * entry(GAIN_ROW + 1)).astype(BF16), qkv_ref[...])
+        factor = row_factor(latents)
         allowed = allowed_ref[...]
         if windows > 1:
             cut = jnp.where(pl.program_id(0) == windows - 1, 1.0, 0.0)
             allowed = 1.0 - cut * (1.0 - allowed)
-        queries = jnp.concatenate([projected[:, :HALF], projected[:, HALF:D]], axis=0)
-        mean_square = mm((queries * queries).astype(BF16), ones_ref[...])
-        twice = jnp.concatenate([factor, factor], axis=0)
-        query_scale = lax.rsqrt(twice * twice * mean_square + head_eps)
-        query_scale = query_scale * (twice * SCORE_SCALE)
+        allowed = jnp.concatenate([allowed, allowed], axis=1)
+        win_queries = projected[:, :D]
         win_keys = projected[:, D : 2 * D] * factor
-        win_values = projected[:, 2 * D :] * factor
-        mixed = []
-        for pair in range(HEADS // 2):
-            half, at = pair // 2, (pair % 2) * PAIR
-            rows = slice(half * TOKENS, (half + 1) * TOKENS)
-            query = queries[rows, at : at + PAIR].astype(BF16)
-            key = win_keys[:, pair * PAIR : (pair + 1) * PAIR]
-            value = win_values[:, pair * PAIR : (pair + 1) * PAIR]
-            key = jnp.concatenate([jnp.where(low, key, 0.0), jnp.where(low, 0.0, key)], axis=0)
-            value = jnp.concatenate(
-                [jnp.where(low, value, 0.0), jnp.where(low, 0.0, value)], axis=0
-            ).astype(BF16)
-            key_square = mm_t(each, (key * key).astype(BF16))[:1]
-            scale = query_scale[rows, at : at + PAIR] * lax.rsqrt(key_square + head_eps)
-            weights = jnp.exp2(mm_t(query, key.astype(BF16)) * scale) * allowed
-            both = mm(weights.astype(BF16), jnp.concatenate([value, half_ref[...]], axis=1))
-            mixed.append((both[:, :PAIR] / both[:, PAIR:]).astype(BF16))
+        win_values = projected[:, 2 * D :] * (factor * (1.0 / HEAD_DIM))
+        halves = [slice(i * HALF, (i + 1) * HALF) for i in range(2)]
+
+        def apart(rows):
+            return jnp.concatenate(
+                [jnp.where(half_head == h, rows, 0.0) for h in range(HEADS // 2)], axis=0
+            )
+
+        keys = [apart(win_keys[:, half]) for half in halves]
+        scores = [
+            mm_t(win_queries[:, half].astype(BF16), key.astype(BF16))
+            for half, key in zip(halves, keys)
+        ]
+        queries = jnp.concatenate([win_queries[:, half] for half in halves], axis=0)
+        query_square = mm((queries * queries).astype(BF16), ones_ref[...])
+        key_squares = [mm_t(each, (key * key).astype(BF16))[:1] for key in keys]
+        values = [
+            jnp.concatenate([apart(win_values[:, half]).astype(BF16), ones_ref[...]], axis=1)
+            for half in halves
+        ]
+        weights = []
+        for i in range(2):
+            square = query_square[i * TOKENS : (i + 1) * TOKENS]
+            scale = lax.rsqrt(factor * factor * square + head_eps) * (factor * SCORE_SCALE)
+            scale = scale * lax.rsqrt(key_squares[i] + head_eps)
+            weights.append((jnp.exp2(scores[i] * scale) * allowed).astype(BF16))
+        both = [mm(weights[i], values[i]) for i in range(2)]
+        mixed = [(each_both[:, :HALF] / each_both[:, HALF:]).astype(BF16) for each_both in both]
         attended = latents + mm(jnp.concatenate(mixed, axis=1), proj_ref[...])
-        normed, factor = layer_norm(attended, entry(GAIN_ROW + 2))
         wait(turn_index, 2, 3)
-        hidden = gelu(mm(normed, up_ref[...]) * factor).astype(BF16)
+        centred = centre(attended)
+        hidden = mm((centred * entry(GAIN_ROW + 2)).astype(BF16), up_ref[...])
+        hidden = gelu(hidden * row_factor(centred)).astype(BF16)
         backbone = attended + mm(hidden, down_ref[...])
         first, second = backbone[:PATCHES], backbone[PATCHES:]
         blended = jnp.concatenate(
             [mixing(l, 0) * first + mixing(l, 1) * second + embed(l) for l in range(LEV)], axis=0
         )
-        normed, factor = layer_norm(blended, entry(GAIN_ROW + 3))
-        current = (current + mm(normed, dec_ref[...]) * factor).astype(BF16).astype(F32)
+        centred = centre(blended)
+        added = mm((centred * entry(GAIN_ROW + 3)).astype(BF16), dec_ref[...])
+        current = (current + added * row_factor(centred)).astype(BF16).astype(F32)
 
     for l in range(LEV):
         wide[:, l * PIN : (l + 1) * PIN] = current[l * PATCHES : (l + 1) * PATCHES]

time: 36.3 us -> 36 us (level)
  no operation moved by 1% of the time
where the time goes in v6:
time: 36 us; the launch traced here: 35.7 us
  Pallas kernels  12.2 us (34%)
  blocking collectives  10.7 us (30%)
  starting transfers between devices  7.39 us (21%)
  waiting for transfers between devices  5.49 us (15%)
    all_to_all x1, blocking collectives, shards(): home = lax.all_to_all(done, 'lon', split_axis=0, concat_axis=0, tiled=True)  10.7 us
    all_to_all x1, starting transfers between devices, shards(): lax.all_to_all(outgoing, 'lon', split_axis=0, concat_axis=0, tiled=True)  7.39 us
    pallas_call x1, Pallas kernels, forecast(): pl.pallas_call(functools.partial(forecast_kernel, windows), grid=grid, in...  7.11 us
    all_to_all x1, waiting for transfers between devices, shards(): lax.all_to_all(outgoing, 'lon', split_axis=0, concat_axis=0, tiled=True)  5.49 us
    pallas_call x2, Pallas kernels, turn(): pl.pallas_call(functools.partial(turn_kernel, step, direction), out_shape...  3.13 us
    pallas_call x1, Pallas kernels, load(): pl.pallas_call(load_kernel, in_specs=[far] * (len(inputs) + 1), out_specs...  1.91 us
  transfers between devices with their start and end apart: 1, of which 1 were waited for; matrix products, arithmetic and copies ran while one was open for 0% of the time, Pallas kernels for 5%

profile of v6, /device:TPU:0, one launch (start us, length us, event | category | flops | bytes accessed | tf_op | source)
XLA Modules:
  0.0 35.7 jit_solution(10577153362791877588)
XLA Ops:
  0.0 1.6 %shard_map.163 = (bf16[16,2,1500]{2,1,0:T(2,128)(2,1)}, f32[8,128]{1,0:T(8,128)}) custom-call(bf16[32,1500]{1,0:T(8,128)(2,1)} %bitcast.13), custom_call_target="tpu_custom_call" | custom-call | tf_op jit(solution)/shard_map/pallas_call | solution.py:398
  1.6 7.4 %all-to-all-start = ((bf16[16,2,1500]{2,1,0:T(2,128)(2,1)}), bf16[16,2,1500]{2,1,0:T(2,128)(2,1)S(1)}, u32[]{:S(2)}, u32[]{:S(2)}) async-start(bf16[16,2,1500]{2,1,0:T(2,128)(2,1)} %get-tuple-element.28), calls=%async_computation | async-start | bytes 196608 | tf_op jit(solution)/shard_map/all_to_all | solution.py:443
  9.0 1.9 %shard_map.164 = (f32[16,512]{1,0:T(8,128)S(1)}, bf16[512,128]{1,0:T(8,128)(2,1)S(1)}, bf16[512,128]{1,0:T(8,128)(2,1)S(1)}, bf16[16,1024]{1,0:T(8,128)(2,1)S(1)...) custom-call(s32[3]{0:T(128)} %refs_0_.1, ...), custom_call_target="tpu_custom_call" | custom-call | bytes 8000000 | tf_op jit(solution)/shard_map/pallas_call | solution.py:184
  10.9 5.5 %all-to-all-done = bf16[16,2,1500]{2,1,0:T(2,128)(2,1)S(1)} async-done(((bf16[16,2,1500]{2,1,0:T(2,128)(2,1)}), bf16[16,2,1500]{2,1,0:T(2,128)(2,1)S(1)}, u32[]{:S(2)}, u32[]{:S(2)}) %all-to-all-start) | async-done | bytes 96032 | tf_op jit(solution)/shard_map/all_to_all | solution.py:443
  16.4 7.1 %shard_map.165 = bf16[1,16,2,1500]{3,2,1,0:T(2,128)(2,1)S(1)} custom-call(f32[16,512]{1,0:T(8,128)S(1)} %get-tuple-element.18.refs_0_, bf16[512,128]{1,0:T(8,128)(2,1)S(1)} %get-tuple-element.19.refs_1_, bf16[512,128]{1,0:T(8,128)(2,1)S(1)} %get-tuple-element.20.refs_2_, bf16[16,1024]{1,0:T(8,128)(2,1)S(1)} %get-tuple-element.21.refs_3_, ...), custom_call_target="tpu_custom_call" | custom-call | tf_op jit(solution)/shard_map/pallas_call | solution.py:364
  23.5 10.7 %all_to_all.10.x_ref = bf16[16,2,1500]{2,1,0:T(2,128)(2,1)} all-to-all(bf16[16,2,1500]{2,1,0:T(2,128)(2,1)S(1)} %bitcast.11), channel_id=1, replica_groups=mesh['groups'=2,'lon'=16] {'lon'}, dimensions={0} | all-to-all | bytes 192000 | tf_op jit(solution)/shard_map/all_to_all | solution.py:454
  34.2 1.6 %shard_map.166 = bf16[32,1500]{1,0:T(8,128)(2,1)} custom-call(bf16[16,2,1500]{2,1,0:T(2,128)(2,1)} %all_to_all.10.x_ref), custom_call_target="tpu_custom_call" | custom-call | tf_op jit(solution)/shard_map/pallas_call | solution.py:398
Async XLA Ops:
  1.6 14.8 %all-to-all-start = ((bf16[16,2,1500]{2,1,0:T(2,128)(2,1)}), bf16[16,2,1500]{2,1,0:T(2,128)(2,1)S(1)}, u32[]{:S(2)}, u32[]{:S(2)}) async-start(bf16[16,2,1500]{2,1,0:T(2,128)(2,1)} %get-tuple-element.28), calls=%async_computation | async-start | bytes 196608 | tf_op jit(solution)/shard_map/all_to_all | solution.py:443

commit v7 on v6

--- a/solution.py
+++ b/solution.py
@@ -26,6 +26,7 @@
 EARLY, LATE = 10, 4
 LANES = 128
 LOAD_LIMIT = 56 * 1024 * 1024
+TURN_LIMIT = 16 * 1024 * 1024
 MAIN_LIMIT = 56 * 1024 * 1024
 EMBED_ROW, MIX_ROW, LATENT_ROW, GAIN_ROW, TABLE_ROWS = 0, 3, 9, 11, 16
 
@@ -183,7 +184,7 @@
     inputs = (*scalars, *rows, dec, *early)
     return pl.pallas_call(
         load_kernel,
-        in_specs=[far] * (len(inputs) + 1),
+        in_specs=[far] * len(inputs) + [pl.BlockSpec(memory_space=pltpu.VMEM)],
         out_specs=[pl.BlockSpec(memory_space=pltpu.VMEM)] * len(made),
         out_shape=made,
         scratch_shapes=[pltpu.SMEM(a.shape, a.dtype) for a in scalars]
@@ -198,7 +199,7 @@
         ],
         compiler_params=pltpu.CompilerParams(vmem_limit_bytes=LOAD_LIMIT),
         cost_estimate=pl.CostEstimate(flops=0, bytes_accessed=8_000_000, transcendentals=0),
-    )(*inputs, after)
+    )(*inputs, pltpu.with_memory_space_constraint(after, pltpu.VMEM))
 
 
 def forecast_kernel(windows, *refs):
@@ -332,10 +333,11 @@
         both = [mm(weights[i], values[i]) for i in range(2)]
         mixed = [(each_both[:, :HALF] / each_both[:, HALF:]).astype(BF16) for each_both in both]
         attended = latents + mm(jnp.concatenate(mixed, axis=1), proj_ref[...])
-        wait(turn_index, 2, 3)
+        wait(turn_index, 2)
         centred = centre(attended)
         hidden = mm((centred * entry(GAIN_ROW + 2)).astype(BF16), up_ref[...])
         hidden = gelu(hidden * row_factor(centred)).astype(BF16)
+        wait(turn_index, 3)
         backbone = attended + mm(hidden, down_ref[...])
         first, second = backbone[:PATCHES], backbone[PATCHES:]
         blended = jnp.concatenate(
@@ -391,12 +393,17 @@
         out_ref[...] = jnp.stack(blocks).reshape(out_ref.shape)
 
 
-def turn(array, shape, step, direction, token=False):
-    shapes = [jax.ShapeDtypeStruct(shape, BF16)]
+def turn(array, shape, step, direction, near=False, token=False):
+    if near and not token:
+        array = pltpu.with_memory_space_constraint(array, pltpu.VMEM)
+    held = near and token
+    shapes = [pltpu.VMEM(shape, BF16) if held else jax.ShapeDtypeStruct(shape, BF16)]
     if token:
-        shapes.append(jax.ShapeDtypeStruct((8, LANES), F32))
+        shapes.append(pltpu.VMEM((8, LANES), F32))
     return pl.pallas_call(
-        functools.partial(turn_kernel, step, direction), out_shape=shapes
+        functools.partial(turn_kernel, step, direction),
+        out_shape=shapes,
+        compiler_params=pltpu.CompilerParams(vmem_limit_bytes=TURN_LIMIT),
     )(array)
 
 
@@ -436,7 +443,7 @@
         dec_gain.reshape(1, D),
     )
     outgoing, token = turn(
-        fields.reshape(local_count, width), (devices, piece_cols, width), cut, 1, token=True
+        fields.reshape(local_count, width), (devices, piece_cols, width), cut, 1, bands == 1, token=True
     )
     early = load(token, scalars, rows, dec_weight.T, (embed_weight, kv_weight, pool_out))
     late = (qkv_weight, attn_proj, mlp_up, mlp_down)
@@ -452,7 +459,7 @@
         done = jnp.roll(done, W_LAT // 2, axis=1)
     done = done.reshape(devices, piece_cols, width)
     home = lax.all_to_all(done, "lon", split_axis=0, concat_axis=0, tiled=True)
-    (forecast_here,) = turn(home, (local_count, width), cut, -1)
+    (forecast_here,) = turn(home, (local_count, width), cut, -1, bands == 1)
     return forecast_here.reshape(fields.shape)
 
 

time: 36 us -> 34.2 us (0.950)
  Pallas kernels: 12.2 us -> 10.1 us
  local copies, waits for them, and re-layouts: 0 us -> 0.89 us
  blocking collectives: 10.7 us -> 9.99 us
    pallas_call x2, Pallas kernels: 3.13 us -> 1.34 us  [turn(): pl.pallas_call(functools.partial(turn_kernel, step, direction), out_shape...]
    unnamed x0 -> x2, local copies, waits for them, and re-layouts: none -> 0.89 us
    all_to_all x1, blocking collectives: 10.7 us -> 9.99 us  [shards(): home = lax.all_to_all(done, 'lon', split_axis=0, concat_axis=0, tiled=True)]
  transfers between devices with their start and end apart: 1 -> 1, of which waited for: 1 -> 1; matrix products, arithmetic and copies ran while one was open for 0% -> 0% of each run, Pallas kernels for 5% -> 6%
where the time goes in v7:
time: 34.2 us; the launch traced here: 33.9 us
  Pallas kernels  10.1 us (30%)
  blocking collectives  9.99 us (29%)
  starting transfers between devices  7.39 us (22%)
  waiting for transfers between devices  5.49 us (16%)
  local copies, waits for them, and re-layouts  0.89 us (3%)
    all_to_all x1, blocking collectives, shards(): home = lax.all_to_all(done, 'lon', split_axis=0, concat_axis=0, tiled=True)  9.99 us
    all_to_all x1, starting transfers between devices, shards(): lax.all_to_all(outgoing, 'lon', split_axis=0, concat_axis=0, tiled=True)  7.39 us
    pallas_call x1, Pallas kernels, forecast(): pl.pallas_call(functools.partial(forecast_kernel, windows), grid=grid, in...  6.84 us
    all_to_all x1, waiting for transfers between devices, shards(): lax.all_to_all(outgoing, 'lon', split_axis=0, concat_axis=0, tiled=True)  5.49 us
    pallas_call x1, Pallas kernels, load(): pl.pallas_call(load_kernel, in_specs=[far] * len(inputs) + [pl.BlockSpec(...  1.91 us
    pallas_call x2, Pallas kernels, turn(): pl.pallas_call(functools.partial(turn_kernel, step, direction), out_shape...  1.34 us
    unnamed x2, local copies, waits for them, and re-layouts  0.89 us
  transfers between devices with their start and end apart: 1, of which 1 were waited for; matrix products, arithmetic and copies ran while one was open for 0% of the time, Pallas kernels for 6%

profile of v7, /device:TPU:0, one launch (start us, length us, event | category | flops | bytes accessed | tf_op | source)
XLA Modules:
  0.0 33.9 jit_solution(6225002444330405702)
XLA Ops:
  0.0 0.0 copy-start
  0.0 0.9 %copy-done = bf16[1,32,1500]{2,1,0:T(8,128)(2,1)S(1)} copy-done((bf16[1,32,1500]{2,1,0:T(8,128)(2,1)S(1)}, bf16[1,32,1500]{2,1,0:T(8,128)(2,1)}, u32[]{:S(2)}) %copy-start) | copy-done | bytes 96024
  0.9 0.7 %shard_map.163 = (bf16[16,2,1500]{2,1,0:T(2,128)(2,1)}, f32[8,128]{1,0:T(8,128)S(1)}) custom-call(bf16[32,1500]{1,0:T(8,128)(2,1)S(1)} %bitcast.12), custom_call_target="tpu_custom_call" | custom-call | tf_op jit(solution)/shard_map/pallas_call | solution.py:403
  1.6 7.4 %all-to-all-start = ((bf16[16,2,1500]{2,1,0:T(2,128)(2,1)}), bf16[16,2,1500]{2,1,0:T(2,128)(2,1)S(1)}, u32[]{:S(2)}, u32[]{:S(2)}) async-start(bf16[16,2,1500]{2,1,0:T(2,128)(2,1)} %get-tuple-element.28), calls=%async_computation | async-start | bytes 196608 | tf_op jit(solution)/shard_map/all_to_all | solution.py:450
  9.0 1.9 %shard_map.164 = (f32[16,512]{1,0:T(8,128)S(1)}, bf16[512,128]{1,0:T(8,128)(2,1)S(1)}, bf16[512,128]{1,0:T(8,128)(2,1)S(1)}, bf16[16,1024]{1,0:T(8,128)(2,1)S(1)...) custom-call(s32[3]{0:T(128)} %refs_0_.1, ...), custom_call_target="tpu_custom_call" | custom-call | bytes 8000000 | tf_op jit(solution)/shard_map/pallas_call | solution.py:185
  10.9 5.5 %all-to-all-done = bf16[16,2,1500]{2,1,0:T(2,128)(2,1)S(1)} async-done(((bf16[16,2,1500]{2,1,0:T(2,128)(2,1)}), bf16[16,2,1500]{2,1,0:T(2,128)(2,1)S(1)}, u32[]{:S(2)}, u32[]{:S(2)}) %all-to-all-start) | async-done | bytes 96032 | tf_op jit(solution)/shard_map/all_to_all | solution.py:450
  16.4 6.8 %shard_map.165 = bf16[1,16,2,1500]{3,2,1,0:T(2,128)(2,1)S(1)} custom-call(f32[16,512]{1,0:T(8,128)S(1)} %get-tuple-element.18.refs_0_, bf16[512,128]{1,0:T(8,128)(2,1)S(1)} %get-tuple-element.19.refs_1_, bf16[512,128]{1,0:T(8,128)(2,1)S(1)} %get-tuple-element.20.refs_2_, bf16[16,1024]{1,0:T(8,128)(2,1)S(1)} %get-tuple-element.21.refs_3_, ...), custom_call_target="tpu_custom_call" | custom-call | tf_op jit(solution)/shard_map/pallas_call | solution.py:366
  23.2 10.0 %all_to_all.10.x_ref = bf16[16,2,1500]{2,1,0:T(2,128)(2,1)S(1)} all-to-all(bf16[16,2,1500]{2,1,0:T(2,128)(2,1)S(1)} %bitcast.11), channel_id=1, replica_groups=mesh['groups'=2,'lon'=16] {'lon'}, dimensions={0} | all-to-all | bytes 192000 | tf_op jit(solution)/shard_map/all_to_all | solution.py:461
  33.2 0.7 %shard_map.166 = bf16[32,1500]{1,0:T(8,128)(2,1)} custom-call(bf16[16,2,1500]{2,1,0:T(2,128)(2,1)S(1)} %all_to_all.10.x_ref), custom_call_target="tpu_custom_call" | custom-call | tf_op jit(solution)/shard_map/pallas_call | solution.py:403
Async XLA Ops:
  0.0 0.9 %copy-start = (bf16[1,32,1500]{2,1,0:T(8,128)(2,1)S(1)}, bf16[1,32,1500]{2,1,0:T(8,128)(2,1)}, u32[]{:S(2)}) copy-start(bf16[1,32,1500]{2,1,0:T(8,128)(2,1)} %param.17) | copy-start | bytes 288004
  1.6 14.8 %all-to-all-start = ((bf16[16,2,1500]{2,1,0:T(2,128)(2,1)}), bf16[16,2,1500]{2,1,0:T(2,128)(2,1)S(1)}, u32[]{:S(2)}, u32[]{:S(2)}) async-start(bf16[16,2,1500]{2,1,0:T(2,128)(2,1)} %get-tuple-element.28), calls=%async_computation | async-start | bytes 196608 | tf_op jit(solution)/shard_map/all_to_all | solution.py:450

commit v8 on v7

--- a/solution.py
+++ b/solution.py
@@ -294,7 +294,7 @@
             ],
             axis=0,
         )
-        wait(turn_index, 0, 1)
+        wait(turn_index, 0)
         projected = mm((latents * entry(GAIN_ROW + 1)).astype(BF16), qkv_ref[...])
         factor = row_factor(latents)
         allowed = allowed_ref[...]
@@ -332,6 +332,7 @@
             weights.append((jnp.exp2(scores[i] * scale) * allowed).astype(BF16))
         both = [mm(weights[i], values[i]) for i in range(2)]
         mixed = [(each_both[:, :HALF] / each_both[:, HALF:]).astype(BF16) for each_both in both]
+        wait(turn_index, 1)
         attended = latents + mm(jnp.concatenate(mixed, axis=1), proj_ref[...])
         wait(turn_index, 2)
         centred = centre(attended)
@@ -403,7 +404,7 @@
     return pl.pallas_call(
         functools.partial(turn_kernel, step, direction),
         out_shape=shapes,
-        compiler_params=pltpu.CompilerParams(vmem_limit_bytes=TURN_LIMIT),
+        compiler_params=pltpu.CompilerParams(vmem_limit_bytes=None if token else TURN_LIMIT),
     )(array)
 
 

time: 34.2 us -> 34.1 us (level)
  Pallas kernels: 10.1 us -> 11 us
  local copies, waits for them, and re-layouts: 0.89 us -> 0 us
    pallas_call x2, Pallas kernels: 1.34 us -> 2.24 us  [turn(): pl.pallas_call(functools.partial(turn_kernel, step, direction), out_shape...]
    unnamed x2 -> x0, local copies, waits for them, and re-layouts: 0.89 us -> none
where the time goes in v8:
time: 34.1 us; the launch traced here: 33.8 us
  Pallas kernels  11 us (32%)
  blocking collectives  9.99 us (29%)
  starting transfers between devices  7.39 us (22%)
  waiting for transfers between devices  5.49 us (16%)
    all_to_all x1, blocking collectives, shards(): home = lax.all_to_all(done, 'lon', split_axis=0, concat_axis=0, tiled=True)  9.99 us
    all_to_all x1, starting transfers between devices, shards(): lax.all_to_all(outgoing, 'lon', split_axis=0, concat_axis=0, tiled=True)  7.39 us
    pallas_call x1, Pallas kernels, forecast(): pl.pallas_call(functools.partial(forecast_kernel, windows), grid=grid, in...  6.81 us
    all_to_all x1, waiting for transfers between devices, shards(): lax.all_to_all(outgoing, 'lon', split_axis=0, concat_axis=0, tiled=True)  5.49 us
    pallas_call x2, Pallas kernels, turn(): pl.pallas_call(functools.partial(turn_kernel, step, direction), out_shape...  2.24 us
    pallas_call x1, Pallas kernels, load(): pl.pallas_call(load_kernel, in_specs=[far] * len(inputs) + [pl.BlockSpec(...  1.91 us
  transfers between devices with their start and end apart: 1, of which 1 were waited for; matrix products, arithmetic and copies ran while one was open for 0% of the time, Pallas kernels for 6%

profile of v8, /device:TPU:0, one launch (start us, length us, event | category | flops | bytes accessed | tf_op | source)
XLA Modules:
  0.0 33.8 jit_solution(15940761883755473659)
XLA Ops:
  0.0 1.6 %shard_map.163 = (bf16[16,2,1500]{2,1,0:T(2,128)(2,1)}, f32[8,128]{1,0:T(8,128)S(1)}) custom-call(bf16[32,1500]{1,0:T(8,128)(2,1)} %bitcast.13), custom_call_target="tpu_custom_call" | custom-call | tf_op jit(solution)/shard_map/pallas_call | solution.py:404
  1.6 7.4 %all-to-all-start = ((bf16[16,2,1500]{2,1,0:T(2,128)(2,1)}), bf16[16,2,1500]{2,1,0:T(2,128)(2,1)S(1)}, u32[]{:S(2)}, u32[]{:S(2)}) async-start(bf16[16,2,1500]{2,1,0:T(2,128)(2,1)} %get-tuple-element.28), calls=%async_computation | async-start | bytes 196608 | tf_op jit(solution)/shard_map/all_to_all | solution.py:451
  9.0 1.9 %shard_map.164 = (f32[16,512]{1,0:T(8,128)S(1)}, bf16[512,128]{1,0:T(8,128)(2,1)S(1)}, bf16[512,128]{1,0:T(8,128)(2,1)S(1)}, bf16[16,1024]{1,0:T(8,128)(2,1)S(1)...) custom-call(s32[3]{0:T(128)} %refs_0_.1, ...), custom_call_target="tpu_custom_call" | custom-call | bytes 8000000 | tf_op jit(solution)/shard_map/pallas_call | solution.py:185
  10.9 5.5 %all-to-all-done = bf16[16,2,1500]{2,1,0:T(2,128)(2,1)S(1)} async-done(((bf16[16,2,1500]{2,1,0:T(2,128)(2,1)}), bf16[16,2,1500]{2,1,0:T(2,128)(2,1)S(1)}, u32[]{:S(2)}, u32[]{:S(2)}) %all-to-all-start) | async-done | bytes 96032 | tf_op jit(solution)/shard_map/all_to_all | solution.py:451
  16.4 6.8 %shard_map.165 = bf16[1,16,2,1500]{3,2,1,0:T(2,128)(2,1)S(1)} custom-call(f32[16,512]{1,0:T(8,128)S(1)} %get-tuple-element.18.refs_0_, bf16[512,128]{1,0:T(8,128)(2,1)S(1)} %get-tuple-element.19.refs_1_, bf16[512,128]{1,0:T(8,128)(2,1)S(1)} %get-tuple-element.20.refs_2_, bf16[16,1024]{1,0:T(8,128)(2,1)S(1)} %get-tuple-element.21.refs_3_, ...), custom_call_target="tpu_custom_call" | custom-call | tf_op jit(solution)/shard_map/pallas_call | solution.py:367
  23.2 10.0 %all_to_all.10.x_ref = bf16[16,2,1500]{2,1,0:T(2,128)(2,1)S(1)} all-to-all(bf16[16,2,1500]{2,1,0:T(2,128)(2,1)S(1)} %bitcast.11), channel_id=1, replica_groups=mesh['groups'=2,'lon'=16] {'lon'}, dimensions={0} | all-to-all | bytes 192000 | tf_op jit(solution)/shard_map/all_to_all | solution.py:462
  33.2 0.7 %shard_map.166 = bf16[32,1500]{1,0:T(8,128)(2,1)} custom-call(bf16[16,2,1500]{2,1,0:T(2,128)(2,1)S(1)} %all_to_all.10.x_ref), custom_call_target="tpu_custom_call" | custom-call | tf_op jit(solution)/shard_map/pallas_call | solution.py:404
Async XLA Ops:
  1.6 14.8 %all-to-all-start = ((bf16[16,2,1500]{2,1,0:T(2,128)(2,1)}), bf16[16,2,1500]{2,1,0:T(2,128)(2,1)S(1)}, u32[]{:S(2)}, u32[]{:S(2)}) async-start(bf16[16,2,1500]{2,1,0:T(2,128)(2,1)} %get-tuple-element.28), calls=%async_computation | async-start | bytes 196608 | tf_op jit(solution)/shard_map/all_to_all | solution.py:451

commit v9 on v8

--- a/solution.py
+++ b/solution.py
@@ -25,6 +25,7 @@
 PAIR = 2 * HEAD_DIM
 EARLY, LATE = 10, 4
 LANES = 128
+CHUNK = 16
 LOAD_LIMIT = 56 * 1024 * 1024
 TURN_LIMIT = 16 * 1024 * 1024
 MAIN_LIMIT = 56 * 1024 * 1024
@@ -243,7 +244,7 @@
         if turn_index == 0:
             in_first_window(action)
 
-    start(0, 1, 2, 3)
+    start(0, 1)
 
     def entry(at):
         return table_ref[at : at + 1, :]
@@ -262,6 +263,8 @@
         [arrived[:, l * PIN : (l + 1) * PIN] for l in range(LEV)], axis=0
     )
 
+    start(2)
+
     def by_level(values):
         return [values[l * PATCHES : (l + 1) * PATCHES] for l in range(LEV)]
 
@@ -269,6 +272,8 @@
         tokens = by_level(mm(current.astype(BF16), embed_ref[...]))
         tokens = jnp.concatenate([tokens[l] + embed(l) for l in range(LEV)], axis=0)
         keyval = mm((tokens * entry(GAIN_ROW)).astype(BF16), kv_ref[...])
+        if turn_index == 0:
+            start(3)
         factor = row_factor(tokens)
         keys = keyval[:, :D]
         values = by_level(keyval[:, D:])
@@ -379,32 +384,56 @@
     )(*early, *late, arranged)
 
 
-def turn_kernel(step, direction, x_ref, out_ref, *token_ref):
-    for ref in token_ref:
-        ref[...] = jnp.zeros_like(ref)
+def turn_out_kernel(step, x_ref, out_ref, token_ref, near, arrivals):
+    count, size = out_ref.shape[:2]
+    copies = [
+        pltpu.make_async_copy(
+            x_ref.at[pl.ds(i * CHUNK, CHUNK)], near.at[pl.ds(i * CHUNK, CHUNK)], arrivals.at[i]
+        )
+        for i in range(count * size // CHUNK)
+    ]
+    for copy in copies:
+        copy.start()
+    token_ref[...] = jnp.zeros_like(token_ref)
     shift = jnp.where(lax.axis_index("lon") < step, 1, 0)
-    if direction > 0:
-        count = out_ref.shape[0]
-        blocks = x_ref[...].reshape(out_ref.shape)
-        for i in range(count):
-            out_ref[lax.rem(i + count - shift, count)] = blocks[i]
-    else:
-        count = x_ref.shape[0]
-        blocks = [x_ref[lax.rem(i + count - shift, count)] for i in range(count)]
-        out_ref[...] = jnp.stack(blocks).reshape(out_ref.shape)
-
-
-def turn(array, shape, step, direction, near=False, token=False):
-    if near and not token:
+    blocks = CHUNK // size
+    for i, copy in enumerate(copies):
+        copy.wait()
+        piece = near[i * CHUNK : (i + 1) * CHUNK, :].reshape((blocks,) + out_ref.shape[1:])
+        for j in range(blocks):
+            out_ref[lax.rem(i * blocks + j + count - shift, count)] = piece[j]
+
+
+def turn_back_kernel(step, x_ref, out_ref):
+    count = x_ref.shape[0]
+    shift = jnp.where(lax.axis_index("lon") < step, 1, 0)
+    blocks = [x_ref[lax.rem(i + count - shift, count)] for i in range(count)]
+    out_ref[...] = jnp.stack(blocks).reshape(out_ref.shape)
+
+
+def turn_out(array, shape, step, near):
+    return pl.pallas_call(
+        functools.partial(turn_out_kernel, step),
+        in_specs=[pl.BlockSpec(memory_space=pl.ANY)],
+        out_shape=[
+            pltpu.VMEM(shape, BF16) if near else jax.ShapeDtypeStruct(shape, BF16),
+            pltpu.VMEM((8, LANES), F32),
+        ],
+        out_specs=[pl.BlockSpec(memory_space=pltpu.VMEM)] * 2,
+        scratch_shapes=[
+            pltpu.VMEM(array.shape, BF16),
+            pltpu.SemaphoreType.DMA((array.shape[0] // CHUNK,)),
+        ],
+    )(array)
+
+
+def turn_back(array, shape, step, near):
+    if near:
         array = pltpu.with_memory_space_constraint(array, pltpu.VMEM)
-    held = near and token
-    shapes = [pltpu.VMEM(shape, BF16) if held else jax.ShapeDtypeStruct(shape, BF16)]
-    if token:
-        shapes.append(pltpu.VMEM((8, LANES), F32))
     return pl.pallas_call(
-        functools.partial(turn_kernel, step, direction),
-        out_shape=shapes,
-        compiler_params=pltpu.CompilerParams(vmem_limit_bytes=None if token else TURN_LIMIT),
+        functools.partial(turn_back_kernel, step),
+        out_shape=jax.ShapeDtypeStruct(shape, BF16),
+        compiler_params=pltpu.CompilerParams(vmem_limit_bytes=TURN_LIMIT),
     )(array)
 
 
@@ -443,8 +472,8 @@
         mlp_gain.reshape(1, D),
         dec_gain.reshape(1, D),
     )
-    outgoing, token = turn(
-        fields.reshape(local_count, width), (devices, piece_cols, width), cut, 1, bands == 1, token=True
+    outgoing, token = turn_out(
+        fields.reshape(local_count, width), (devices, piece_cols, width), cut, bands == 1
     )
     early = load(token, scalars, rows, dec_weight.T, (embed_weight, kv_weight, pool_out))
     late = (qkv_weight, attn_proj, mlp_up, mlp_down)
@@ -460,7 +489,7 @@
         done = jnp.roll(done, W_LAT // 2, axis=1)
     done = done.reshape(devices, piece_cols, width)
     home = lax.all_to_all(done, "lon", split_axis=0, concat_axis=0, tiled=True)
-    (forecast_here,) = turn(home, (local_count, width), cut, -1, bands == 1)
+    forecast_here = turn_back(home, (local_count, width), cut, bands == 1)
     return forecast_here.reshape(fields.shape)
 
 

time: 34.1 us -> 34.1 us (level)
  no operation moved by 1% of the time
where the time goes in v9:
time: 34.1 us; the launch traced here: 33.8 us
  Pallas kernels  10.9 us (32%)
  blocking collectives  9.99 us (29%)
  starting transfers between devices  7.4 us (22%)
  waiting for transfers between devices  5.49 us (16%)
    all_to_all x1, blocking collectives, shards(): home = lax.all_to_all(done, 'lon', split_axis=0, concat_axis=0, tiled=True)  9.99 us
    all_to_all x1, starting transfers between devices, shards(): lax.all_to_all(outgoing, 'lon', split_axis=0, concat_axis=0, tiled=True)  7.4 us
    pallas_call x1, Pallas kernels, forecast(): pl.pallas_call(functools.partial(forecast_kernel, windows), grid=grid, in...  6.8 us
    all_to_all x1, waiting for transfers between devices, shards(): lax.all_to_all(outgoing, 'lon', split_axis=0, concat_axis=0, tiled=True)  5.49 us
    pallas_call x1, Pallas kernels, load(): pl.pallas_call(load_kernel, in_specs=[far] * len(inputs) + [pl.BlockSpec(...  1.91 us
    pallas_call x1, Pallas kernels, turn_out(): pl.pallas_call(functools.partial(turn_out_kernel, step), in_specs=[pl.Blo...  1.49 us
  transfers between devices with their start and end apart: 1, of which 1 were waited for; matrix products, arithmetic and copies ran while one was open for 0% of the time, Pallas kernels for 6%

profile of v9, /device:TPU:0, one launch (start us, length us, event | category | flops | bytes accessed | tf_op | source)
XLA Modules:
  0.0 33.8 jit_solution(13486801733296447105)
XLA Ops:
  0.0 1.5 %shard_map.163 = (bf16[16,2,1500]{2,1,0:T(2,128)(2,1)}, f32[8,128]{1,0:T(8,128)S(1)}) custom-call(bf16[32,1500]{1,0:T(8,128)(2,1)} %bitcast.13), custom_call_target="tpu_custom_call" | custom-call | tf_op jit(solution)/shard_map/pallas_call | solution.py:415
  1.5 7.4 %all-to-all-start = ((bf16[16,2,1500]{2,1,0:T(2,128)(2,1)}), bf16[16,2,1500]{2,1,0:T(2,128)(2,1)S(1)}, u32[]{:S(2)}, u32[]{:S(2)}) async-start(bf16[16,2,1500]{2,1,0:T(2,128)(2,1)} %get-tuple-element.28), calls=%async_computation | async-start | bytes 196608 | tf_op jit(solution)/shard_map/all_to_all | solution.py:480
  8.9 1.9 %shard_map.164 = (f32[16,512]{1,0:T(8,128)S(1)}, bf16[512,128]{1,0:T(8,128)(2,1)S(1)}, bf16[512,128]{1,0:T(8,128)(2,1)S(1)}, bf16[16,1024]{1,0:T(8,128)(2,1)S(1)...) custom-call(s32[3]{0:T(128)} %refs_0_.1, ...), custom_call_target="tpu_custom_call" | custom-call | bytes 8000000 | tf_op jit(solution)/shard_map/pallas_call | solution.py:186
  10.8 5.5 %all-to-all-done = bf16[16,2,1500]{2,1,0:T(2,128)(2,1)S(1)} async-done(((bf16[16,2,1500]{2,1,0:T(2,128)(2,1)}), bf16[16,2,1500]{2,1,0:T(2,128)(2,1)S(1)}, u32[]{:S(2)}, u32[]{:S(2)}) %all-to-all-start) | async-done | bytes 96032 | tf_op jit(solution)/shard_map/all_to_all | solution.py:480
  16.3 6.8 %shard_map.165 = bf16[1,16,2,1500]{3,2,1,0:T(2,128)(2,1)S(1)} custom-call(f32[16,512]{1,0:T(8,128)S(1)} %get-tuple-element.18.refs_0_, bf16[512,128]{1,0:T(8,128)(2,1)S(1)} %get-tuple-element.19.refs_1_, bf16[512,128]{1,0:T(8,128)(2,1)S(1)} %get-tuple-element.20.refs_2_, bf16[16,1024]{1,0:T(8,128)(2,1)S(1)} %get-tuple-element.21.refs_3_, ...), custom_call_target="tpu_custom_call" | custom-call | tf_op jit(solution)/shard_map/pallas_call | solution.py:372
  23.1 10.0 %all_to_all.10.x_ref = bf16[16,2,1500]{2,1,0:T(2,128)(2,1)S(1)} all-to-all(bf16[16,2,1500]{2,1,0:T(2,128)(2,1)S(1)} %bitcast.11), channel_id=1, replica_groups=mesh['groups'=2,'lon'=16] {'lon'}, dimensions={0} | all-to-all | bytes 192000 | tf_op jit(solution)/shard_map/all_to_all | solution.py:491
  33.1 0.7 %shard_map.166 = bf16[32,1500]{1,0:T(8,128)(2,1)} custom-call(bf16[16,2,1500]{2,1,0:T(2,128)(2,1)S(1)} %all_to_all.10.x_ref), custom_call_target="tpu_custom_call" | custom-call | tf_op jit(solution)/shard_map/pallas_call | solution.py:433
Async XLA Ops:
  1.5 14.8 %all-to-all-start = ((bf16[16,2,1500]{2,1,0:T(2,128)(2,1)}), bf16[16,2,1500]{2,1,0:T(2,128)(2,1)S(1)}, u32[]{:S(2)}, u32[]{:S(2)}) async-start(bf16[16,2,1500]{2,1,0:T(2,128)(2,1)} %get-tuple-element.28), calls=%async_computation | async-start | bytes 196608 | tf_op jit(solution)/shard_map/all_to_all | solution.py:480

commit v10 on v9

--- a/solution.py
+++ b/solution.py
@@ -341,10 +341,15 @@
         attended = latents + mm(jnp.concatenate(mixed, axis=1), proj_ref[...])
         wait(turn_index, 2)
         centred = centre(attended)
-        hidden = mm((centred * entry(GAIN_ROW + 2)).astype(BF16), up_ref[...])
-        hidden = gelu(hidden * row_factor(centred)).astype(BF16)
+        normed = (centred * entry(GAIN_ROW + 2)).astype(BF16)
+        units = [slice(i * MLP // 2, (i + 1) * MLP // 2) for i in range(2)]
+        hidden = [mm(normed, up_ref[:, unit]) for unit in units]
+        factor = row_factor(centred)
+        first = gelu(hidden[0] * factor).astype(BF16)
         wait(turn_index, 3)
-        backbone = attended + mm(hidden, down_ref[...])
+        first = mm(first, down_ref[units[0], :])
+        second = gelu(hidden[1] * factor).astype(BF16)
+        backbone = attended + first + mm(second, down_ref[units[1], :])
         first, second = backbone[:PATCHES], backbone[PATCHES:]
         blended = jnp.concatenate(
             [mixing(l, 0) * first + mixing(l, 1) * second + embed(l) for l in range(LEV)], axis=0

time: 34.1 us -> 34.1 us (level)
  no operation moved by 1% of the time
where the time goes in v10:
time: 34.1 us; the launch traced here: 33.8 us
  Pallas kernels  10.8 us (32%)
  blocking collectives  9.99 us (29%)
  starting transfers between devices  7.4 us (22%)
  waiting for transfers between devices  5.49 us (16%)
    all_to_all x1, blocking collectives, shards(): home = lax.all_to_all(done, 'lon', split_axis=0, concat_axis=0, tiled=True)  9.99 us
    all_to_all x1, starting transfers between devices, shards(): lax.all_to_all(outgoing, 'lon', split_axis=0, concat_axis=0, tiled=True)  7.4 us
    pallas_call x1, Pallas kernels, forecast(): pl.pallas_call(functools.partial(forecast_kernel, windows), grid=grid, in...  6.77 us
    all_to_all x1, waiting for transfers between devices, shards(): lax.all_to_all(outgoing, 'lon', split_axis=0, concat_axis=0, tiled=True)  5.49 us
    pallas_call x1, Pallas kernels, load(): pl.pallas_call(load_kernel, in_specs=[far] * len(inputs) + [pl.BlockSpec(...  1.91 us
    pallas_call x1, Pallas kernels, turn_out(): pl.pallas_call(functools.partial(turn_out_kernel, step), in_specs=[pl.Blo...  1.49 us
  transfers between devices with their start and end apart: 1, of which 1 were waited for; matrix products, arithmetic and copies ran while one was open for 0% of the time, Pallas kernels for 6%

profile of v10, /device:TPU:0, one launch (start us, length us, event | category | flops | bytes accessed | tf_op | source)
XLA Modules:
  0.0 33.8 jit_solution(2689624470264190800)
XLA Ops:
  0.0 1.5 %shard_map.163 = (bf16[16,2,1500]{2,1,0:T(2,128)(2,1)}, f32[8,128]{1,0:T(8,128)S(1)}) custom-call(bf16[32,1500]{1,0:T(8,128)(2,1)} %bitcast.13), custom_call_target="tpu_custom_call" | custom-call | tf_op jit(solution)/shard_map/pallas_call | solution.py:420
  1.5 7.4 %all-to-all-start = ((bf16[16,2,1500]{2,1,0:T(2,128)(2,1)}), bf16[16,2,1500]{2,1,0:T(2,128)(2,1)S(1)}, u32[]{:S(2)}, u32[]{:S(2)}) async-start(bf16[16,2,1500]{2,1,0:T(2,128)(2,1)} %get-tuple-element.28), calls=%async_computation | async-start | bytes 196608 | tf_op jit(solution)/shard_map/all_to_all | solution.py:485
  8.9 1.9 %shard_map.164 = (f32[16,512]{1,0:T(8,128)S(1)}, bf16[512,128]{1,0:T(8,128)(2,1)S(1)}, bf16[512,128]{1,0:T(8,128)(2,1)S(1)}, bf16[16,1024]{1,0:T(8,128)(2,1)S(1)...) custom-call(s32[3]{0:T(128)} %refs_0_.1, ...), custom_call_target="tpu_custom_call" | custom-call | bytes 8000000 | tf_op jit(solution)/shard_map/pallas_call | solution.py:186
  10.8 5.5 %all-to-all-done = bf16[16,2,1500]{2,1,0:T(2,128)(2,1)S(1)} async-done(((bf16[16,2,1500]{2,1,0:T(2,128)(2,1)}), bf16[16,2,1500]{2,1,0:T(2,128)(2,1)S(1)}, u32[]{:S(2)}, u32[]{:S(2)}) %all-to-all-start) | async-done | bytes 96032 | tf_op jit(solution)/shard_map/all_to_all | solution.py:485
  16.3 6.8 %shard_map.165 = bf16[1,16,2,1500]{3,2,1,0:T(2,128)(2,1)S(1)} custom-call(f32[16,512]{1,0:T(8,128)S(1)} %get-tuple-element.18.refs_0_, bf16[512,128]{1,0:T(8,128)(2,1)S(1)} %get-tuple-element.19.refs_1_, bf16[512,128]{1,0:T(8,128)(2,1)S(1)} %get-tuple-element.20.refs_2_, bf16[16,1024]{1,0:T(8,128)(2,1)S(1)} %get-tuple-element.21.refs_3_, ...), custom_call_target="tpu_custom_call" | custom-call | tf_op jit(solution)/shard_map/pallas_call | solution.py:377
  23.1 10.0 %all_to_all.10.x_ref = bf16[16,2,1500]{2,1,0:T(2,128)(2,1)S(1)} all-to-all(bf16[16,2,1500]{2,1,0:T(2,128)(2,1)S(1)} %bitcast.11), channel_id=1, replica_groups=mesh['groups'=2,'lon'=16] {'lon'}, dimensions={0} | all-to-all | bytes 192000 | tf_op jit(solution)/shard_map/all_to_all | solution.py:496
  33.1 0.7 %shard_map.166 = bf16[32,1500]{1,0:T(8,128)(2,1)} custom-call(bf16[16,2,1500]{2,1,0:T(2,128)(2,1)S(1)} %all_to_all.10.x_ref), custom_call_target="tpu_custom_call" | custom-call | tf_op jit(solution)/shard_map/pallas_call | solution.py:438
Async XLA Ops:
  1.5 14.8 %all-to-all-start = ((bf16[16,2,1500]{2,1,0:T(2,128)(2,1)}), bf16[16,2,1500]{2,1,0:T(2,128)(2,1)S(1)}, u32[]{:S(2)}, u32[]{:S(2)}) async-start(bf16[16,2,1500]{2,1,0:T(2,128)(2,1)} %get-tuple-element.28), calls=%async_computation | async-start | bytes 196608 | tf_op jit(solution)/shard_map/all_to_all | solution.py:485

commit v11 on v10

--- a/solution.py
+++ b/solution.py
@@ -277,8 +277,12 @@
         factor = row_factor(tokens)
         keys = keyval[:, :D]
         values = by_level(keyval[:, D:])
-        scores = mm(keys.astype(BF16), query_ref[...])[:, : LATL * HEADS]
-        mean_square = mm((keys * keys).astype(BF16), mean_ref[...])[:, : LATL * HEADS]
+        stacked = jnp.concatenate([keys.astype(BF16), (keys * keys).astype(BF16)], axis=0)
+        tables = jnp.concatenate([query_ref[...], mean_ref[...]], axis=1)
+        found = mm(stacked, tables)
+        rows = LEV * PATCHES
+        scores = found[:rows, : LATL * HEADS]
+        mean_square = found[rows:, LANES : LANES + LATL * HEADS]
         scale = factor * lax.rsqrt(factor * factor * mean_square + head_eps)
         parts = by_level(jnp.exp2(scores * (scale * SCORE_SCALE)))
         inverse = 1.0 / (parts[0] + parts[1] + parts[2])

time: 34.1 us -> 34.1 us (level)
  no operation moved by 1% of the time
where the time goes in v11:
time: 34.1 us; the launch traced here: 33.8 us
  Pallas kernels  10.9 us (32%)
  blocking collectives  9.99 us (29%)
  starting transfers between devices  7.4 us (22%)
  waiting for transfers between devices  5.49 us (16%)
    all_to_all x1, blocking collectives, shards(): home = lax.all_to_all(done, 'lon', split_axis=0, concat_axis=0, tiled=True)  9.99 us
    all_to_all x1, starting transfers between devices, shards(): lax.all_to_all(outgoing, 'lon', split_axis=0, concat_axis=0, tiled=True)  7.4 us
    pallas_call x1, Pallas kernels, forecast(): pl.pallas_call(functools.partial(forecast_kernel, windows), grid=grid, in...  6.82 us
    all_to_all x1, waiting for transfers between devices, shards(): lax.all_to_all(outgoing, 'lon', split_axis=0, concat_axis=0, tiled=True)  5.49 us
    pallas_call x1, Pallas kernels, load(): pl.pallas_call(load_kernel, in_specs=[far] * len(inputs) + [pl.BlockSpec(...  1.91 us
    pallas_call x1, Pallas kernels, turn_out(): pl.pallas_call(functools.partial(turn_out_kernel, step), in_specs=[pl.Blo...  1.49 us
  transfers between devices with their start and end apart: 1, of which 1 were waited for; matrix products, arithmetic and copies ran while one was open for 0% of the time, Pallas kernels for 6%

profile of v11, /device:TPU:0, one launch (start us, length us, event | category | flops | bytes accessed | tf_op | source)
XLA Modules:
  0.0 33.8 jit_solution(11696479323356407726)
XLA Ops:
  0.0 1.5 %shard_map.163 = (bf16[16,2,1500]{2,1,0:T(2,128)(2,1)}, f32[8,128]{1,0:T(8,128)S(1)}) custom-call(bf16[32,1500]{1,0:T(8,128)(2,1)} %bitcast.13), custom_call_target="tpu_custom_call" | custom-call | tf_op jit(solution)/shard_map/pallas_call | solution.py:424
  1.5 7.4 %all-to-all-start = ((bf16[16,2,1500]{2,1,0:T(2,128)(2,1)}), bf16[16,2,1500]{2,1,0:T(2,128)(2,1)S(1)}, u32[]{:S(2)}, u32[]{:S(2)}) async-start(bf16[16,2,1500]{2,1,0:T(2,128)(2,1)} %get-tuple-element.28), calls=%async_computation | async-start | bytes 196608 | tf_op jit(solution)/shard_map/all_to_all | solution.py:489
  8.9 1.9 %shard_map.164 = (f32[16,512]{1,0:T(8,128)S(1)}, bf16[512,128]{1,0:T(8,128)(2,1)S(1)}, bf16[512,128]{1,0:T(8,128)(2,1)S(1)}, bf16[16,1024]{1,0:T(8,128)(2,1)S(1)...) custom-call(s32[3]{0:T(128)} %refs_0_.1, ...), custom_call_target="tpu_custom_call" | custom-call | bytes 8000000 | tf_op jit(solution)/shard_map/pallas_call | solution.py:186
  10.8 5.5 %all-to-all-done = bf16[16,2,1500]{2,1,0:T(2,128)(2,1)S(1)} async-done(((bf16[16,2,1500]{2,1,0:T(2,128)(2,1)}), bf16[16,2,1500]{2,1,0:T(2,128)(2,1)S(1)}, u32[]{:S(2)}, u32[]{:S(2)}) %all-to-all-start) | async-done | bytes 96032 | tf_op jit(solution)/shard_map/all_to_all | solution.py:489
  16.3 6.8 %shard_map.165 = bf16[1,16,2,1500]{3,2,1,0:T(2,128)(2,1)S(1)} custom-call(f32[16,512]{1,0:T(8,128)S(1)} %get-tuple-element.18.refs_0_, bf16[512,128]{1,0:T(8,128)(2,1)S(1)} %get-tuple-element.19.refs_1_, bf16[512,128]{1,0:T(8,128)(2,1)S(1)} %get-tuple-element.20.refs_2_, bf16[16,1024]{1,0:T(8,128)(2,1)S(1)} %get-tuple-element.21.refs_3_, ...), custom_call_target="tpu_custom_call" | custom-call | tf_op jit(solution)/shard_map/pallas_call | solution.py:381
  23.1 10.0 %all_to_all.10.x_ref = bf16[16,2,1500]{2,1,0:T(2,128)(2,1)S(1)} all-to-all(bf16[16,2,1500]{2,1,0:T(2,128)(2,1)S(1)} %bitcast.11), channel_id=1, replica_groups=mesh['groups'=2,'lon'=16] {'lon'}, dimensions={0} | all-to-all | bytes 192000 | tf_op jit(solution)/shard_map/all_to_all | solution.py:500
  33.1 0.7 %shard_map.166 = bf16[32,1500]{1,0:T(8,128)(2,1)} custom-call(bf16[16,2,1500]{2,1,0:T(2,128)(2,1)S(1)} %all_to_all.10.x_ref), custom_call_target="tpu_custom_call" | custom-call | tf_op jit(solution)/shard_map/pallas_call | solution.py:442
Async XLA Ops:
  1.5 14.8 %all-to-all-start = ((bf16[16,2,1500]{2,1,0:T(2,128)(2,1)}), bf16[16,2,1500]{2,1,0:T(2,128)(2,1)S(1)}, u32[]{:S(2)}, u32[]{:S(2)}) async-start(bf16[16,2,1500]{2,1,0:T(2,128)(2,1)} %get-tuple-element.28), calls=%async_computation | async-start | bytes 196608 | tf_op jit(solution)/shard_map/all_to_all | solution.py:489

commit v12 on v11

--- a/solution.py
+++ b/solution.py
@@ -217,7 +217,7 @@
         pool_ref,
     ) = refs[:EARLY]
     far, (x_ref, out_ref), refs = refs[EARLY:][:LATE], refs[EARLY + LATE :][:2], refs[EARLY + LATE + 2 :]
-    near, (wide, arrivals) = refs[:LATE], refs[LATE:]
+    near, (arrivals,) = refs[:LATE], refs[LATE:]
     qkv_ref, proj_ref, up_ref, down_ref = near
     copies = [
         pltpu.make_async_copy(far[i], near[i], arrivals.at[i]) for i in range(LATE)
@@ -362,9 +362,8 @@
         added = mm((centred * entry(GAIN_ROW + 3)).astype(BF16), dec_ref[...])
         current = (current + added * row_factor(centred)).astype(BF16).astype(F32)
 
-    for l in range(LEV):
-        wide[:, l * PIN : (l + 1) * PIN] = current[l * PATCHES : (l + 1) * PATCHES]
-    out_ref[0] = wide[...].astype(BF16).reshape(out_ref.shape[1:])
+    wide = jnp.concatenate(by_level(current), axis=1)
+    out_ref[0] = wide.astype(BF16).reshape(out_ref.shape[1:])
 
 
 def forecast(windows, arranged, early, late):
@@ -385,10 +384,7 @@
         out_specs=block,
         out_shape=result,
         scratch_shapes=[pltpu.VMEM(a.shape, a.dtype) for a in late]
-        + [
-            pltpu.VMEM((PATCHES, LEV * PIN), F32),
-            pltpu.SemaphoreType.DMA((LATE,)),
-        ],
+        + [pltpu.SemaphoreType.DMA((LATE,))],
         compiler_params=pltpu.CompilerParams(vmem_limit_bytes=MAIN_LIMIT),
     )(*early, *late, arranged)
 

time: 34.1 us -> 34.1 us (level)
  no operation moved by 1% of the time
where the time goes in v12:
time: 34.1 us; the launch traced here: 33.8 us
  Pallas kernels  10.9 us (32%)
  blocking collectives  9.99 us (29%)
  starting transfers between devices  7.4 us (22%)
  waiting for transfers between devices  5.49 us (16%)
    all_to_all x1, blocking collectives, shards(): home = lax.all_to_all(done, 'lon', split_axis=0, concat_axis=0, tiled=True)  9.99 us
    all_to_all x1, starting transfers between devices, shards(): lax.all_to_all(outgoing, 'lon', split_axis=0, concat_axis=0, tiled=True)  7.4 us
    pallas_call x1, Pallas kernels, forecast(): pl.pallas_call(functools.partial(forecast_kernel, windows), grid=grid, in...  6.81 us
    all_to_all x1, waiting for transfers between devices, shards(): lax.all_to_all(outgoing, 'lon', split_axis=0, concat_axis=0, tiled=True)  5.49 us
    pallas_call x1, Pallas kernels, load(): pl.pallas_call(load_kernel, in_specs=[far] * len(inputs) + [pl.BlockSpec(...  1.91 us
    pallas_call x1, Pallas kernels, turn_out(): pl.pallas_call(functools.partial(turn_out_kernel, step), in_specs=[pl.Blo...  1.49 us
  transfers between devices with their start and end apart: 1, of which 1 were waited for; matrix products, arithmetic and copies ran while one was open for 0% of the time, Pallas kernels for 6%

profile of v12, /device:TPU:0, one launch (start us, length us, event | category | flops | bytes accessed | tf_op | source)
XLA Modules:
  0.0 33.8 jit_solution(16979805060467314379)
XLA Ops:
  0.0 1.5 %shard_map.163 = (bf16[16,2,1500]{2,1,0:T(2,128)(2,1)}, f32[8,128]{1,0:T(8,128)S(1)}) custom-call(bf16[32,1500]{1,0:T(8,128)(2,1)} %bitcast.13), custom_call_target="tpu_custom_call" | custom-call | tf_op jit(solution)/shard_map/pallas_call | solution.py:420
  1.5 7.4 %all-to-all-start = ((bf16[16,2,1500]{2,1,0:T(2,128)(2,1)}), bf16[16,2,1500]{2,1,0:T(2,128)(2,1)S(1)}, u32[]{:S(2)}, u32[]{:S(2)}) async-start(bf16[16,2,1500]{2,1,0:T(2,128)(2,1)} %get-tuple-element.28), calls=%async_computation | async-start | bytes 196608 | tf_op jit(solution)/shard_map/all_to_all | solution.py:485
  8.9 1.9 %shard_map.164 = (f32[16,512]{1,0:T(8,128)S(1)}, bf16[512,128]{1,0:T(8,128)(2,1)S(1)}, bf16[512,128]{1,0:T(8,128)(2,1)S(1)}, bf16[16,1024]{1,0:T(8,128)(2,1)S(1)...) custom-call(s32[3]{0:T(128)} %refs_0_.1, ...), custom_call_target="tpu_custom_call" | custom-call | bytes 8000000 | tf_op jit(solution)/shard_map/pallas_call | solution.py:186
  10.8 5.5 %all-to-all-done = bf16[16,2,1500]{2,1,0:T(2,128)(2,1)S(1)} async-done(((bf16[16,2,1500]{2,1,0:T(2,128)(2,1)}), bf16[16,2,1500]{2,1,0:T(2,128)(2,1)S(1)}, u32[]{:S(2)}, u32[]{:S(2)}) %all-to-all-start) | async-done | bytes 96032 | tf_op jit(solution)/shard_map/all_to_all | solution.py:485
  16.3 6.8 %shard_map.165 = bf16[1,16,2,1500]{3,2,1,0:T(2,128)(2,1)S(1)} custom-call(f32[16,512]{1,0:T(8,128)S(1)} %get-tuple-element.18.refs_0_, bf16[512,128]{1,0:T(8,128)(2,1)S(1)} %get-tuple-element.19.refs_1_, bf16[512,128]{1,0:T(8,128)(2,1)S(1)} %get-tuple-element.20.refs_2_, bf16[16,1024]{1,0:T(8,128)(2,1)S(1)} %get-tuple-element.21.refs_3_, ...), custom_call_target="tpu_custom_call" | custom-call | tf_op jit(solution)/shard_map/pallas_call | solution.py:380
  23.1 10.0 %all_to_all.10.x_ref = bf16[16,2,1500]{2,1,0:T(2,128)(2,1)S(1)} all-to-all(bf16[16,2,1500]{2,1,0:T(2,128)(2,1)S(1)} %bitcast.11), channel_id=1, replica_groups=mesh['groups'=2,'lon'=16] {'lon'}, dimensions={0} | all-to-all | bytes 192000 | tf_op jit(solution)/shard_map/all_to_all | solution.py:496
  33.1 0.7 %shard_map.166 = bf16[32,1500]{1,0:T(8,128)(2,1)} custom-call(bf16[16,2,1500]{2,1,0:T(2,128)(2,1)S(1)} %all_to_all.10.x_ref), custom_call_target="tpu_custom_call" | custom-call | tf_op jit(solution)/shard_map/pallas_call | solution.py:438
Async XLA Ops:
  1.5 14.8 %all-to-all-start = ((bf16[16,2,1500]{2,1,0:T(2,128)(2,1)}), bf16[16,2,1500]{2,1,0:T(2,128)(2,1)S(1)}, u32[]{:S(2)}, u32[]{:S(2)}) async-start(bf16[16,2,1500]{2,1,0:T(2,128)(2,1)} %get-tuple-element.28), calls=%async_computation | async-start | bytes 196608 | tf_op jit(solution)/shard_map/all_to_all | solution.py:485

commit v13 on v12

--- a/solution.py
+++ b/solution.py
@@ -345,15 +345,10 @@
         attended = latents + mm(jnp.concatenate(mixed, axis=1), proj_ref[...])
         wait(turn_index, 2)
         centred = centre(attended)
-        normed = (centred * entry(GAIN_ROW + 2)).astype(BF16)
-        units = [slice(i * MLP // 2, (i + 1) * MLP // 2) for i in range(2)]
-        hidden = [mm(normed, up_ref[:, unit]) for unit in units]
-        factor = row_factor(centred)
-        first = gelu(hidden[0] * factor).astype(BF16)
+        hidden = mm((centred * entry(GAIN_ROW + 2)).astype(BF16), up_ref[...])
+        hidden = gelu(hidden * row_factor(centred)).astype(BF16)
         wait(turn_index, 3)
-        first = mm(first, down_ref[units[0], :])
-        second = gelu(hidden[1] * factor).astype(BF16)
-        backbone = attended + first + mm(second, down_ref[units[1], :])
+        backbone = attended + mm(hidden, down_ref[...])
         first, second = backbone[:PATCHES], backbone[PATCHES:]
         blended = jnp.concatenate(
             [mixing(l, 0) * first + mixing(l, 1) * second + embed(l) for l in range(LEV)], axis=0

time: 34.1 us -> 34.1 us (level)
  no operation moved by 1% of the time
where the time goes in v13:
time: 34.1 us; the launch traced here: 33.8 us
  Pallas kernels  10.9 us (32%)
  blocking collectives  9.99 us (29%)
  starting transfers between devices  7.4 us (22%)
  waiting for transfers between devices  5.49 us (16%)
    all_to_all x1, blocking collectives, shards(): home = lax.all_to_all(done, 'lon', split_axis=0, concat_axis=0, tiled=True)  9.99 us
    all_to_all x1, starting transfers between devices, shards(): lax.all_to_all(outgoing, 'lon', split_axis=0, concat_axis=0, tiled=True)  7.4 us
    pallas_call x1, Pallas kernels, forecast(): pl.pallas_call(functools.partial(forecast_kernel, windows), grid=grid, in...  6.84 us
    all_to_all x1, waiting for transfers between devices, shards(): lax.all_to_all(outgoing, 'lon', split_axis=0, concat_axis=0, tiled=True)  5.49 us
    pallas_call x1, Pallas kernels, load(): pl.pallas_call(load_kernel, in_specs=[far] * len(inputs) + [pl.BlockSpec(...  1.91 us
    pallas_call x1, Pallas kernels, turn_out(): pl.pallas_call(functools.partial(turn_out_kernel, step), in_specs=[pl.Blo...  1.49 us
  transfers between devices with their start and end apart: 1, of which 1 were waited for; matrix products, arithmetic and copies ran while one was open for 0% of the time, Pallas kernels for 6%

profile of v13, /device:TPU:0, one launch (start us, length us, event | category | flops | bytes accessed | tf_op | source)
XLA Modules:
  0.0 33.8 jit_solution(1098120801545683463)
XLA Ops:
  0.0 1.5 %shard_map.163 = (bf16[16,2,1500]{2,1,0:T(2,128)(2,1)}, f32[8,128]{1,0:T(8,128)S(1)}) custom-call(bf16[32,1500]{1,0:T(8,128)(2,1)} %bitcast.13), custom_call_target="tpu_custom_call" | custom-call | tf_op jit(solution)/shard_map/pallas_call | solution.py:415
  1.5 7.4 %all-to-all-start = ((bf16[16,2,1500]{2,1,0:T(2,128)(2,1)}), bf16[16,2,1500]{2,1,0:T(2,128)(2,1)S(1)}, u32[]{:S(2)}, u32[]{:S(2)}) async-start(bf16[16,2,1500]{2,1,0:T(2,128)(2,1)} %get-tuple-element.28), calls=%async_computation | async-start | bytes 196608 | tf_op jit(solution)/shard_map/all_to_all | solution.py:480
  8.9 1.9 %shard_map.164 = (f32[16,512]{1,0:T(8,128)S(1)}, bf16[512,128]{1,0:T(8,128)(2,1)S(1)}, bf16[512,128]{1,0:T(8,128)(2,1)S(1)}, bf16[16,1024]{1,0:T(8,128)(2,1)S(1)...) custom-call(s32[3]{0:T(128)} %refs_0_.1, ...), custom_call_target="tpu_custom_call" | custom-call | bytes 8000000 | tf_op jit(solution)/shard_map/pallas_call | solution.py:186
  10.8 5.5 %all-to-all-done = bf16[16,2,1500]{2,1,0:T(2,128)(2,1)S(1)} async-done(((bf16[16,2,1500]{2,1,0:T(2,128)(2,1)}), bf16[16,2,1500]{2,1,0:T(2,128)(2,1)S(1)}, u32[]{:S(2)}, u32[]{:S(2)}) %all-to-all-start) | async-done | bytes 96032 | tf_op jit(solution)/shard_map/all_to_all | solution.py:480
  16.3 6.8 %shard_map.165 = bf16[1,16,2,1500]{3,2,1,0:T(2,128)(2,1)S(1)} custom-call(f32[16,512]{1,0:T(8,128)S(1)} %get-tuple-element.18.refs_0_, bf16[512,128]{1,0:T(8,128)(2,1)S(1)} %get-tuple-element.19.refs_1_, bf16[512,128]{1,0:T(8,128)(2,1)S(1)} %get-tuple-element.20.refs_2_, bf16[16,1024]{1,0:T(8,128)(2,1)S(1)} %get-tuple-element.21.refs_3_, ...), custom_call_target="tpu_custom_call" | custom-call | tf_op jit(solution)/shard_map/pallas_call | solution.py:375
  23.2 10.0 %all_to_all.10.x_ref = bf16[16,2,1500]{2,1,0:T(2,128)(2,1)S(1)} all-to-all(bf16[16,2,1500]{2,1,0:T(2,128)(2,1)S(1)} %bitcast.11), channel_id=1, replica_groups=mesh['groups'=2,'lon'=16] {'lon'}, dimensions={0} | all-to-all | bytes 192000 | tf_op jit(solution)/shard_map/all_to_all | solution.py:491
  33.1 0.7 %shard_map.166 = bf16[32,1500]{1,0:T(8,128)(2,1)} custom-call(bf16[16,2,1500]{2,1,0:T(2,128)(2,1)S(1)} %all_to_all.10.x_ref), custom_call_target="tpu_custom_call" | custom-call | tf_op jit(solution)/shard_map/pallas_call | solution.py:433
Async XLA Ops:
  1.5 14.8 %all-to-all-start = ((bf16[16,2,1500]{2,1,0:T(2,128)(2,1)}), bf16[16,2,1500]{2,1,0:T(2,128)(2,1)S(1)}, u32[]{:S(2)}, u32[]{:S(2)}) async-start(bf16[16,2,1500]{2,1,0:T(2,128)(2,1)} %get-tuple-element.28), calls=%async_computation | async-start | bytes 196608 | tf_op jit(solution)/shard_map/all_to_all | solution.py:480
